TPU v7x, 768 devices: a whole 4x8x12 slice. The times are simulated.
768 devices in a mesh: grp: 8 (over z_hi, x), row: 96 (over y, z_lo, core).
Axes of the slice: x: 4, y: 8, z: 12 (z_hi: 2, z_lo: 6; z = z_hi * 6 + z_lo), core: 2. Of those that a mesh axis runs over, the one named last changes fastest.
Arguments:
- features: bfloat16 [73728, 128], P('row'), may hold values from -6 to 6
- dest_plan: int32 [96, 48], replicated, may hold values from 0 to 95, as said below
- adj_tiles: bfloat16 [24, 768, 73728], P(None, 'grp', 'row'), may hold values from -0.046875 to 0.046875
- tile_cols: int32 [96, 24], P('row'), may hold values from 0 to 95, as said below
- tile_count: int32 [96], P('row'), may hold values from 12 to 24, as said below
- grad_out: bfloat16 [73728, 256], P('row'), may hold values from -0.0234375 to 0.0234375
- weight: bfloat16 [128, 256], replicated, may hold values from -0.5 to 0.5
Outputs:
- hidden_out: bfloat16 [73728, 256], P('row')
- weight_grad: float32 [128, 256], replicated
Inputs may be any that keep to these rules, and one draw needn't show every extreme that they name: `dest_plan`: row s holds 48 different blocks, none equal to s; every block appears exactly 48 times in all. `tile_cols`: each row holds 24 different column blocks. `tile_count`: some row block uses all 24 slots in every draw.
All inputs are finite; a program needn't handle non-finite values.
Results may differ from a plain program's by a relative error of at most 0.0056.
Values may be sent and summed in bfloat16 or wider, within the bound.
No kernel may reach another device: no remote copies, remote signals or barrier semaphores. Data moves between devices by JAX's collectives and lax.ppermute only.
A program may use at most 32 MiB of HBM per device.

v0:
```python
import jax
import jax.numpy as jnp
from jax import lax
from jax.sharding import PartitionSpec as P

KEEP = 576


def contract_rows(first_op, second_op):
    return lax.dot_general(
        first_op, second_op, (((0,), (0,)), ((), ())), preferred_element_type=jnp.float32
    )


def on_device(features, dest_plan, adj_tiles, tile_cols, tile_count, grad_out, weight):
    block_rows, feat_width = features.shape
    row_count = lax.axis_size("row")
    group_count = lax.axis_size("grp")
    own_row = lax.axis_index("row")
    own_group = lax.axis_index("grp")
    leaving = dest_plan.shape[1]
    part_rows = (block_rows - KEEP) // leaving
    slice_rows = block_rows // group_count
    targets = lax.dynamic_index_in_dim(dest_plan, own_row, 0, keepdims=False)
    owners = jnp.arange(row_count, dtype=jnp.int32)
    outgoing = (targets[:, None] == owners[None, :]).astype(jnp.bfloat16)
    leaving_rows = features[KEEP:].reshape(leaving, part_rows * feat_width)
    packed = contract_rows(outgoing, leaving_rows).astype(jnp.bfloat16)
    arrived = lax.all_to_all(packed, "row", split_axis=0, concat_axis=0, tiled=True)
    senders = jnp.any(dest_plan == own_row, axis=1)
    sender_rank = jnp.cumsum(senders.astype(jnp.int32), dtype=jnp.int32) - 1
    positions = jnp.arange(leaving, dtype=jnp.int32)
    chooser = (senders[None, :] & (sender_rank[None, :] == positions[:, None])).astype(jnp.bfloat16)
    incoming = jnp.dot(chooser, arrived, preferred_element_type=jnp.float32).astype(jnp.bfloat16)
    relocated = jnp.concatenate(
        [features[:KEEP], incoming.reshape(leaving * part_rows, feat_width)], axis=0
    )
    own_slice = lax.dynamic_slice_in_dim(relocated, own_group * slice_rows, slice_rows, 0)
    column_ids = tile_cols[0]
    live_slots = jnp.arange(column_ids.shape[0], dtype=jnp.int32) < tile_count[0]
    gathered = lax.all_gather(own_slice[None], "row", axis=0, tiled=True)
    picked = jnp.take(gathered, column_ids, axis=0)
    picked = jnp.where(live_slots[:, None, None], picked, jnp.zeros_like(picked))
    partial_value = lax.dot_general(
        adj_tiles, picked, (((0, 1), (0, 1)), ((), ())), preferred_element_type=jnp.float32
    )
    summed = lax.psum(partial_value, "grp")
    aggregated = summed.astype(jnp.bfloat16)
    projected = jnp.dot(aggregated, weight, preferred_element_type=jnp.float32)
    sigmoid_part = jax.nn.sigmoid(projected)
    activated = (projected * sigmoid_part).astype(jnp.bfloat16)
    slope = sigmoid_part * (1.0 + projected * (1.0 - sigmoid_part))
    masked = (grad_out.astype(jnp.float32) * slope).astype(jnp.bfloat16)
    local_grad = contract_rows(aggregated, masked)
    weight_grad = lax.psum(local_grad, "row")
    return (activated, weight_grad)


def solution(mesh):
    in_specs = (
        P("row", None),
        P(),
        P(None, "grp", "row"),
        P("row", None),
        P("row"),
        P("row", None),
        P(),
    )
    out_specs = (P("row", None), P())
    return jax.shard_map(
        on_device, mesh=mesh, in_specs=in_specs, out_specs=out_specs, check_vma=False
    )
```

profile of v0, /device:TPU:1, one launch (start us, length us, event | category | flops | bytes accessed | tf_op | source)
XLA Modules:
  0.0 1273.7 jit_solution(14168825618092686878)
XLA Ops:
  7.2 0.0 copy-start
  7.2 1.6 slice.7
  8.8 1.5 reshape.85
  10.2 0.9 dynamic-slice_reduce_fusion
  11.1 1.7 fusion
  12.9 0.6 broadcast.61
  13.5 2.3 reduce.4
  15.7 1.6 reshape.100
  17.3 20.1 %all-to-all-start = ((bf16[96,2,256]{2,1,0:T(2,128)(2,1)}), bf16[96,2,256]{2,1,0:T(2,128)(2,1)}, u32[]{:S(2)}, u32[]{:S(2)}) async-start(bf16[96,2,256]{2,1,0:T(2,128)(2,1)} %reshape.100), calls=%async_computation | async-start | bytes 196608 | tf_op jit(solution)/shard_map/all_to_all | solution.py:29
  37.4 0.0 all-gather.3.cloned.1.call-start
  37.5 0.8 compare_reduce_fusion
  38.2 1.6 slice.6
  39.8 0.7 copy.13
  40.5 1.5 reduce-window.8
  42.1 0.9 add_reduce_fusion
  43.0 7.9 all-to-all-done
  50.8 1.6 reshape.101
  52.5 1.7 convolution_convert_fusion.1
  54.2 1.5 reshape.86
  55.6 1.4 fusion.13
  57.0 0.0 all-gather.3.cloned.1.call-update
  57.0 0.0 all-reduce.3.cloned.1.call-start
  57.7 0.7 fusion.19
  58.4 0.7 compare_and_fusion
  59.0 167.4 %all-gather.3.cloned.1.call-done = bf16[9216,128]{1,0:T(8,128)(2,1)} async-done(((bf16[96,128]{1,0:T(8,128)(2,1)}), bf16[9216,128]{1,0:T(8,128)(2,1)}) %all-gather.3.cloned.1.call-update) | async-done | bytes 2359312 | tf_op jit(solution)/shard_map/all_gather | solution.py:41
  226.5 3.1 gather_fusion
  229.6 0.0 copy-done
  229.6 2.7 convolution_bitcast_fusion
  232.4 62.3 %all-reduce.4 = bf16[768,128]{0,1:T(8,128)(2,1)} all-reduce(f32[768,128]{0,1:T(8,128)} %convolution_bitcast_fusion), channel_id=1, replica_groups=mesh['grp'=8,'row'=96] {'grp'}, use_global_device_ids=true, to_apply=%region_2.3 | all-reduce | flops 98304 | bytes 589824 | tf_op jit(solution)/shard_map/psum | solution.py:47
  294.6 0.0 copy-start.1
  294.6 0.0 copy-start.2
  294.6 2.1 multiply_convert_fusion.1
  296.8 0.0 copy-done.1
  296.8 0.0 copy-done.2
  296.8 1.1 fusion.5
  297.9 0.0 all-reduce.3.cloned.1.call-update
  297.9 967.4 %all-reduce.3.cloned.1.call-done = f32[128,256]{1,0:T(8,128)} async-done(((f32[128,256]{1,0:T(8,128)}), f32[128,256]{1,0:T(8,128)}) %all-reduce.3.cloned.1.call-update) | async-done | bytes 131088 | tf_op jit(solution)/shard_map/psum | solution.py:55
  1265.3 1.6 copy.25
  (2 shorter events, 0.0 us)
Async XLA Ops:
  7.2 222.5 %copy-start = (bf16[24,96,768]{2,1,0:T(8,128)(2,1)S(1)}, bf16[24,96,768]{2,1,0:T(8,128)(2,1)}, u32[]{:S(2)}) copy-start(bf16[24,96,768]{2,1,0:T(8,128)(2,1)} %param.9) | copy-start | bytes 10616836
  17.3 33.5 %all-to-all-start = ((bf16[96,2,256]{2,1,0:T(2,128)(2,1)}), bf16[96,2,256]{2,1,0:T(2,128)(2,1)}, u32[]{:S(2)}, u32[]{:S(2)}) async-start(bf16[96,2,256]{2,1,0:T(2,128)(2,1)} %reshape.100), calls=%async_computation | async-start | bytes 196608 | tf_op jit(solution)/shard_map/all_to_all | solution.py:29
  37.4 189.1 %all-gather.3.cloned.1.call-start = ((), (), s32[]{:S(2)}) async-start(), calls=%async_computation.2 | async-start | bytes 2383872 | tf_op jit(solution)/shard_map/all_gather | solution.py:41
  57.0 1208.3 %all-reduce.3.cloned.1.call-start = ((), (), s32[]{:S(2)}) async-start(), calls=%async_computation.1 | async-start | bytes 262144 | tf_op jit(solution)/shard_map/psum | solution.py:55
  294.6 2.2 copy-start.1
  294.6 2.2 copy-start.2
Sparse Core Ops, SparseCore 0:
  57.1 169.3 all-gather.2
  298.0 967.2 all-reduce.2
where the time goes:
time: 1280 us; the launch traced here: 1270 us
  waiting for transfers between devices  1140 us (89%)
  blocking collectives  62.3 us (5%)
  starting transfers between devices  20.2 us (2%)
  local copies, waits for them, and re-layouts  16.2 us (1%)
  between operations  14.7 us (1%)
    psum x1, waiting for transfers between devices, on_device(): weight_grad = lax.psum(local_grad, 'row')  967 us
    all_gather x1, waiting for transfers between devices, on_device(): gathered = lax.all_gather(own_slice[None], 'row', axis=0, tiled=True)  167 us
    psum x1, blocking collectives, on_device(): summed = lax.psum(partial_value, 'grp')  62.3 us
  transfers between devices with their start and end apart: 3, of which 3 were waited for; matrix products, arithmetic and copies ran while one was open for 1% of the time, Pallas kernels for 0%

commit v1 on v0

v1 whole, which is shorter than its diff:
```python
import jax
import jax.numpy as jnp
from jax import lax
from jax.sharding import Mesh, PartitionSpec as P

KEEP = 576
GRP = ("zh", "x")
ROW = ("y", "zl", "c")
CHIPS = ("y", "zl")
FINE = (2, 4, 8, 6, 2)


def exchange(pieces, axes):
    return lax.all_to_all(pieces, axes, split_axis=0, concat_axis=0, tiled=True)


def spread(value, axes):
    copies = jnp.broadcast_to(value[None], (lax.axis_size(axes),) + value.shape)
    return exchange(copies, axes)


def relocate(features, dest_plan, own_row):
    block_rows, feat_width = features.shape
    row_count, leaving = dest_plan.shape
    part_rows = (block_rows - KEEP) // leaving
    targets = lax.dynamic_index_in_dim(dest_plan, own_row, 0, keepdims=False)
    owners = jnp.arange(row_count, dtype=jnp.int32)
    outgoing = (targets[None, :] == owners[:, None]).astype(jnp.bfloat16)
    leaving_rows = features[KEEP:].reshape(leaving, part_rows * feat_width)
    packed = jnp.dot(outgoing, leaving_rows, preferred_element_type=jnp.float32).astype(jnp.bfloat16)
    arrived = exchange(packed, ROW)
    senders = jnp.any(dest_plan == own_row, axis=1)
    sender_rank = jnp.sum(
        (senders[None, :] & (owners[None, :] < owners[:, None])).astype(jnp.int32), axis=1
    )
    positions = jnp.arange(leaving, dtype=jnp.int32)
    chooser = (senders[None, :] & (sender_rank[None, :] == positions[:, None])).astype(jnp.bfloat16)
    incoming = jnp.dot(chooser, arrived, preferred_element_type=jnp.float32).astype(jnp.bfloat16)
    return jnp.concatenate(
        [features[:KEEP], incoming.reshape(leaving * part_rows, feat_width)], axis=0
    )


def on_device(features, dest_plan, adj_tiles, tile_cols, tile_count, grad_out, weight):
    block_rows, feat_width = features.shape
    hid = weight.shape[1]
    group_count = lax.axis_size(GRP)
    own_row = lax.axis_index(ROW)
    own_group = lax.axis_index(GRP)
    own_core = lax.axis_index("c")
    slice_rows = block_rows // group_count
    relocated = relocate(features, dest_plan, own_row)
    own_slice = lax.dynamic_slice_in_dim(relocated, own_group * slice_rows, slice_rows, 0)

    same_core = spread(own_slice, CHIPS).reshape(-1, slice_rows, feat_width)
    other_core = lax.ppermute(same_core, "c", [(0, 1), (1, 0)])
    gathered = jnp.concatenate([same_core, other_core], axis=0)
    column_ids = tile_cols[0]
    places = column_ids // 2 + jnp.where(column_ids % 2 == own_core, 0, same_core.shape[0])
    live_slots = jnp.arange(column_ids.shape[0], dtype=jnp.int32) < tile_count[0]
    picked = jnp.take(gathered, places, axis=0)
    picked = jnp.where(live_slots[:, None, None], picked, jnp.zeros_like(picked))

    partial_value = lax.dot_general(
        picked, adj_tiles, (((0, 1), (0, 1)), ((), ())), preferred_element_type=jnp.float32
    ).astype(jnp.bfloat16)
    terms = exchange(partial_value, GRP).reshape(group_count, -1, block_rows)
    own_feats = jnp.sum(terms.astype(jnp.float32), axis=0).astype(jnp.bfloat16)
    aggregated = spread(own_feats, GRP).reshape(feat_width, block_rows)

    projected = lax.dot_general(
        aggregated, weight, (((0,), (0,)), ((), ())), preferred_element_type=jnp.float32
    )
    sigmoid_part = jax.nn.sigmoid(projected)
    activated = (projected * sigmoid_part).astype(jnp.bfloat16)
    slope = sigmoid_part * (1.0 + projected * (1.0 - sigmoid_part))
    masked = (grad_out.astype(jnp.float32) * slope).astype(jnp.bfloat16)
    local_grad = jnp.dot(own_feats, masked, preferred_element_type=jnp.float32)

    y_terms = exchange(local_grad, "y").reshape(lax.axis_size("y"), -1, hid)
    chip_terms = spread(jnp.sum(y_terms, axis=0), ("zl", "c"))
    own_grad = jnp.sum(chip_terms.reshape((-1,) + y_terms.shape[1:]), axis=0)
    weight_grad = spread(own_grad, GRP + ("y",)).reshape(feat_width, hid)
    return (activated, weight_grad)


def solution(mesh):
    fine_mesh = Mesh(mesh.devices.reshape(FINE), GRP + ROW)
    in_specs = (
        P(ROW, None),
        P(),
        P(None, GRP, ROW),
        P(ROW, None),
        P(ROW),
        P(ROW, None),
        P(),
    )
    out_specs = (P(ROW, None), P())
    return jax.shard_map(
        on_device, mesh=fine_mesh, in_specs=in_specs, out_specs=out_specs, check_vma=False
    )
```

time: 1280 us -> 211 us (0.16)
  waiting for transfers between devices: 1140 us -> 23.4 us
  blocking collectives: 62.3 us -> 116 us
  between operations: 14.7 us -> 1.42 us
    psum x1 -> x0, waiting for transfers between devices: 967 us -> none  [on_device(): weight_grad = lax.psum(local_grad, 'row')]
    all_gather x1 -> x0, waiting for transfers between devices: 167 us -> none  [on_device(): gathered = lax.all_gather(own_slice[None], 'row', axis=0, tiled=True)]
    all_to_all x0 -> x5, blocking collectives: none -> 116 us  [exchange(): return lax.all_to_all(pieces, axes, split_axis=0, concat_axis=0, tiled=True)]
    psum x1 -> x0, blocking collectives: 62.3 us -> none  [on_device(): summed = lax.psum(partial_value, 'grp')]
    all_to_all x1 -> x2, waiting for transfers between devices: 7.87 us -> 21.7 us  [exchange(): return lax.all_to_all(pieces, axes, split_axis=0, concat_axis=0, tiled=True)]
  transfers between devices with their start and end apart: 3 -> 3, of which waited for: 3 -> 3; matrix products, arithmetic and copies ran while one was open for 1% -> 2% of each run, Pallas kernels for 0% -> 0%
where the time goes in v1:
time: 211 us; the launch traced here: 209 us
  blocking collectives  116 us (55%)
  starting transfers between devices  32.4 us (15%)
  waiting for transfers between devices  23.4 us (11%)
  local copies, waits for them, and re-layouts  19.3 us (9%)
  other arithmetic  8.48 us (4%)
  matrix products  7.81 us (4%)
    all_to_all x5, blocking collectives, exchange(): return lax.all_to_all(pieces, axes, split_axis=0, concat_axis=0, tiled=True)  116 us
    all_to_all x2, starting transfers between devices, exchange(): return lax.all_to_all(pieces, axes, split_axis=0, concat_axis=0, tiled=True)  24.1 us
    all_to_all x2, waiting for transfers between devices, exchange(): return lax.all_to_all(pieces, axes, split_axis=0, concat_axis=0, tiled=True)  21.7 us
    ppermute x1, starting transfers between devices, on_device(): other_core = lax.ppermute(same_core, 'c', [(0, 1), (1, 0)])  8.23 us
  transfers between devices with their start and end apart: 3, of which 3 were waited for; matrix products, arithmetic and copies ran while one was open for 2% of the time, Pallas kernels for 0%

profile of v1, /device:TPU:1, one launch (start us, length us, event | category | flops | bytes accessed | tf_op | source)
XLA Modules:
  0.0 209.1 jit_solution(486954983291843729)
XLA Ops:
  0.6 0.0 copy-start
  0.7 1.6 slice.7
  2.2 1.5 reshape.156
  3.7 0.9 dynamic-slice_reduce_fusion
  4.6 1.6 fusion.1
  6.2 0.6 broadcast.193
  6.8 2.3 %reduce.5 = bf16[96,512]{1,0:T(8,128)(2,1)} reduce(bf16[96,1,512]{2,0,1:T(8,128)(2,1)} %fusion.1, bf16[]{:T(256)} %broadcast.193), dimensions={1}, to_apply=%copy.16.reduce_sub_computation | reduce | bytes 196610 | tf_op jit(solution)/shard_map/all_to_all | solution.py:14
  9.1 1.6 reshape.171
  10.6 20.1 %all-to-all-start = ((bf16[96,2,256]{2,1,0:T(2,128)(2,1)}), bf16[96,2,256]{2,1,0:T(2,128)(2,1)}, u32[]{:S(2)}, u32[]{:S(2)}) async-start(bf16[96,2,256]{2,1,0:T(2,128)(2,1)} %reshape.171), calls=%async_computation | async-start | bytes 196608 | tf_op jit(solution)/shard_map/all_to_all | solution.py:14
  30.8 0.0 copy-start.2
  30.8 1.6 slice.6
  32.4 0.8 compare_reduce_fusion
  33.1 0.1 convert_reduce_fusion
  33.2 10.9 %all-to-all-done = bf16[96,2,256]{2,1,0:T(2,128)(2,1)} async-done(((bf16[96,2,256]{2,1,0:T(2,128)(2,1)}), bf16[96,2,256]{2,1,0:T(2,128)(2,1)}, u32[]{:S(2)}, u32[]{:S(2)}) %all-to-all-start) | async-done | bytes 98336 | tf_op jit(solution)/shard_map/all_to_all | solution.py:14
  44.2 1.6 reshape.172
  45.8 1.7 convolution_convert_fusion.1
  47.5 1.5 reshape.157
  49.0 0.8 fusion.13
  49.7 0.2 broadcast_in_dim.39
  49.9 39.2 %all_to_all.47 = bf16[48,96,128]{2,1,0:T(8,128)(2,1)S(1)} all-to-all(bf16[48,96,128]{2,1,0:T(8,128)(2,1)S(1)} %broadcast_in_dim.39), channel_id=1, replica_groups=mesh['zh'=2,'x'=4,'y'=8,'zl'=6,'c'=2] {'y','zl'}, dimensions={0} | all-to-all | bytes 2359296 | tf_op jit(solution)/shard_map/all_to_all | solution.py:14
  89.1 8.2 %collective-permute-start = (bf16[48,96,128]{2,1,0:T(8,128)(2,1)S(1)}, bf16[48,96,128]{2,1,0:T(8,128)(2,1)S(1)}, u32[]{:S(2)}, u32[]{:S(2)}) collective-permute-start(bf16[48,96,128]{2,1,0:T(8,128)(2,1)S(1)} %all_to_all.47), channel_id=1, source_target_pairs={{0,1},{1,0},{2,3},{3,2},{4,5},{5,4},{6,7},{7,6},{8,9},{9,8},{10,11... | collective-permute-start | bytes 3538952 | tf_op jit(solution)/shard_map/ppermute | solution.py:56
  98.0 0.0 copy-done.2
  98.0 1.7 collective-permute-done
  99.8 1.6 pad_maximum_fusion
  101.4 3.1 %gather_fusion = bf16[24,96,128]{2,1,0:T(8,128)(2,1)} fusion(bf16[96,96,128]{2,1,0:T(8,128)(2,1)} %pad_maximum_fusion, s32[1024]{0:T(1024)S(1)} %pad_clamp_fusion), kind=kCustom, calls=%fused_computation | custom fusion | bytes 1179744 | tf_op jit(solution)/shard_map/jit(_take)/gather | solution.py:61
  104.5 0.0 copy-done
  104.5 2.0 fusion
  106.5 25.5 %all_to_all.48 = bf16[8,16,768]{2,1,0:T(8,128)(2,1)} all-to-all(bf16[8,16,768]{2,1,0:T(8,128)(2,1)S(1)} %bitcast.52), channel_id=1, replica_groups=mesh['zh'=2,'x'=4,'y'=8,'zl'=6,'c'=2] {'zh','x'}, dimensions={0} | all-to-all | bytes 393216 | tf_op jit(solution)/shard_map/all_to_all | solution.py:14
  132.0 1.6 reduce_sum.40
  133.6 1.4 broadcast_in_dim.69
  135.0 4.0 %all-to-all-start.3 = ((bf16[8,16,768]{2,1,0:T(8,128)(2,1)}), bf16[8,16,768]{2,1,0:T(8,128)(2,1)}, u32[]{:S(2)}, u32[]{:S(2)}) async-start(bf16[8,16,768]{2,1,0:T(8,128)(2,1)} %broadcast_in_dim.69), calls=%async_computation.3 | async-start | bytes 393216 | tf_op jit(solution)/shard_map/all_to_all | solution.py:14
  139.0 1.4 dot_general.21
  140.4 10.8 %all-to-all-done.3 = bf16[8,16,768]{2,1,0:T(8,128)(2,1)} async-done(((bf16[8,16,768]{2,1,0:T(8,128)(2,1)}), bf16[8,16,768]{2,1,0:T(8,128)(2,1)}, u32[]{:S(2)}, u32[]{:S(2)}) %all-to-all-start.3) | async-done | bytes 196640 | tf_op jit(solution)/shard_map/all_to_all | solution.py:14
  151.1 0.0 copy-start.1
  151.1 0.0 copy-start.3
  151.1 2.1 %multiply_convert_fusion.1 = (bf16[768,256]{1,0:T(8,128)(2,1)}, f32[768,256]{1,0:T(8,128)S(1)}) fusion(bf16[128,768]{1,0:T(8,128)(2,1)} %bitcast.7, bf16[128,256]{1,0:T(8,128)(2,1)} %param.13), kind=kOutput, calls=%fused_computation.8 | convolution fusion | flops 51314688 | bytes 1441792 | tf_op jit(solution)/shard_map/dot_general | solution.py:71
  153.3 0.0 copy-done.1
  153.3 0.0 copy-done.3
  153.3 0.4 fusion.6
  153.7 10.0 %all_to_all.49 = f32[8,2,256]{2,1,0:T(2,128)S(1)} all-to-all(f32[8,2,256]{2,1,0:T(2,128)S(1)} %copy.18), channel_id=1, replica_groups=mesh['zh'=2,'x'=4,'y'=8,'zl'=6,'c'=2] {'y'}, dimensions={0} | all-to-all | bytes 32768 | tf_op jit(solution)/shard_map/all_to_all | solution.py:14
  163.8 0.6 reduce_sum.41
  164.4 0.7 broadcast_in_dim.70
  165.0 21.1 %all_to_all.50 = f32[12,2,256]{2,1,0:T(2,128)} all-to-all(f32[12,2,256]{2,1,0:T(2,128)S(1)} %broadcast_in_dim.70), channel_id=1, replica_groups=mesh['zh'=2,'x'=4,'y'=8,'zl'=6,'c'=2] {'zl','c'}, dimensions={0} | all-to-all | bytes 49152 | tf_op jit(solution)/shard_map/all_to_all | solution.py:14
  186.1 0.8 reduce_sum.42
  186.9 20.5 %all_to_all.51 = f32[64,2,256]{2,1,0:T(2,128)} all-to-all(f32[64,2,256]{2,1,0:T(2,128)S(1)} %broadcast_in_dim.71), channel_id=1, replica_groups=mesh['zh'=2,'x'=4,'y'=8,'zl'=6,'c'=2] {'zh','x','y'}, dimensions={0} | all-to-all | bytes 262144 | tf_op jit(solution)/shard_map/all_to_all | solution.py:14
  207.4 1.6 reshape.159
  (5 shorter events, 0.1 us)
Async XLA Ops:
  0.6 103.9 %copy-start = (bf16[24,96,768]{2,1,0:T(8,128)(2,1)S(1)}, bf16[24,96,768]{2,1,0:T(8,128)(2,1)}, u32[]{:S(2)}) copy-start(bf16[24,96,768]{2,1,0:T(8,128)(2,1)} %param.9) | copy-start | bytes 10616836
  10.6 33.5 %all-to-all-start = ((bf16[96,2,256]{2,1,0:T(2,128)(2,1)}), bf16[96,2,256]{2,1,0:T(2,128)(2,1)}, u32[]{:S(2)}, u32[]{:S(2)}) async-start(bf16[96,2,256]{2,1,0:T(2,128)(2,1)} %reshape.171), calls=%async_computation | async-start | bytes 196608 | tf_op jit(solution)/shard_map/all_to_all | solution.py:14
  30.8 67.2 %copy-start.2 = (s32[1,24]{1,0:T(1,128)S(1)}, s32[1,24]{1,0:T(1,128)}, u32[]{:S(2)}) copy-start(s32[1,24]{1,0:T(1,128)} %param.10) | copy-start | bytes 292
  89.1 10.7 %collective-permute-start = (bf16[48,96,128]{2,1,0:T(8,128)(2,1)S(1)}, bf16[48,96,128]{2,1,0:T(8,128)(2,1)S(1)}, u32[]{:S(2)}, u32[]{:S(2)}) collective-permute-start(bf16[48,96,128]{2,1,0:T(8,128)(2,1)S(1)} %all_to_all.47), channel_id=1, source_target_pairs={{0,1},{1,0},{2,3},{3,2},{4,5},{5,4},{6,7},{7,6},{8,9},{9,8},{10,11... | collective-permute-start | bytes 3538952 | tf_op jit(solution)/shard_map/ppermute | solution.py:56
  135.0 16.1 %all-to-all-start.3 = ((bf16[8,16,768]{2,1,0:T(8,128)(2,1)}), bf16[8,16,768]{2,1,0:T(8,128)(2,1)}, u32[]{:S(2)}, u32[]{:S(2)}) async-start(bf16[8,16,768]{2,1,0:T(8,128)(2,1)} %broadcast_in_dim.69), calls=%async_computation.3 | async-start | bytes 393216 | tf_op jit(solution)/shard_map/all_to_all | solution.py:14
  151.1 2.1 %copy-start.1 = (bf16[8,2,768]{2,1,0:T(2,128)(2,1)S(1)}, bf16[8,2,768]{2,1,0:T(2,128)(2,1)}, u32[]{:S(2)}) copy-start(bf16[8,2,768]{2,1,0:T(2,128)(2,1)} %dot_general.21) | copy-start | bytes 73732
  151.1 2.1 %copy-start.3 = (bf16[768,256]{1,0:T(8,128)(2,1)S(1)}, bf16[768,256]{1,0:T(8,128)(2,1)}, u32[]{:S(2)}) copy-start(bf16[768,256]{1,0:T(8,128)(2,1)} %param.12) | copy-start | bytes 1179652

commit v2 on v1

--- a/solution.py
+++ b/solution.py
@@ -64,9 +64,11 @@
     partial_value = lax.dot_general(
         picked, adj_tiles, (((0, 1), (0, 1)), ((), ())), preferred_element_type=jnp.float32
     ).astype(jnp.bfloat16)
-    terms = exchange(partial_value, GRP).reshape(group_count, -1, block_rows)
-    own_feats = jnp.sum(terms.astype(jnp.float32), axis=0).astype(jnp.bfloat16)
-    aggregated = spread(own_feats, GRP).reshape(feat_width, block_rows)
+    terms = exchange(partial_value, "x").reshape(lax.axis_size("x"), -1, block_rows)
+    near = jnp.sum(terms.astype(jnp.float32), axis=0).astype(jnp.bfloat16)
+    far = lax.ppermute(near, "zh", [(0, 1), (1, 0)])
+    own_feats = (near.astype(jnp.float32) + far.astype(jnp.float32)).astype(jnp.bfloat16)
+    aggregated = spread(own_feats, "x").reshape(feat_width, block_rows)
 
     projected = lax.dot_general(
         aggregated, weight, (((0,), (0,)), ((), ())), preferred_element_type=jnp.float32
@@ -75,12 +77,12 @@
     activated = (projected * sigmoid_part).astype(jnp.bfloat16)
     slope = sigmoid_part * (1.0 + projected * (1.0 - sigmoid_part))
     masked = (grad_out.astype(jnp.float32) * slope).astype(jnp.bfloat16)
-    local_grad = jnp.dot(own_feats, masked, preferred_element_type=jnp.float32)
+    local_grad = jnp.dot(aggregated, masked, preferred_element_type=jnp.float32)
 
-    y_terms = exchange(local_grad, "y").reshape(lax.axis_size("y"), -1, hid)
-    chip_terms = spread(jnp.sum(y_terms, axis=0), ("zl", "c"))
-    own_grad = jnp.sum(chip_terms.reshape((-1,) + y_terms.shape[1:]), axis=0)
-    weight_grad = spread(own_grad, GRP + ("y",)).reshape(feat_width, hid)
+    ring_terms = exchange(local_grad, ("y", "c")).reshape(lax.axis_size(("y", "c")), -1, hid)
+    line_terms = spread(jnp.sum(ring_terms, axis=0), "zl")
+    own_grad = jnp.sum(line_terms.reshape((-1,) + ring_terms.shape[1:]), axis=0)
+    weight_grad = spread(own_grad, ("y", "c")).reshape(feat_width, hid)
     return (activated, weight_grad)
 
 

time: 211 us -> 189 us (0.90)
  blocking collectives: 116 us -> 100 us
  waiting for transfers between devices: 23.4 us -> 14.4 us
  starting transfers between devices: 32.4 us -> 40 us
  local copies, waits for them, and re-layouts: 19.3 us -> 14.8 us
    all_to_all x5 -> x6, blocking collectives: 116 us -> 100 us  [exchange(): return lax.all_to_all(pieces, axes, split_axis=0, concat_axis=0, tiled=True)]
    ppermute x0 -> x1, starting transfers between devices: none -> 11.7 us  [on_device(): far = lax.ppermute(near, 'zh', [(0, 1), (1, 0)])]
    all_to_all x2 -> x1, waiting for transfers between devices: 21.7 us -> 10.9 us  [exchange(): return lax.all_to_all(pieces, axes, split_axis=0, concat_axis=0, tiled=True)]
    all_to_all x2 -> x1, starting transfers between devices: 24.1 us -> 20.1 us  [exchange(): return lax.all_to_all(pieces, axes, split_axis=0, concat_axis=0, tiled=True)]
    broadcast_in_dim x4, local copies, waits for them, and re-layouts: 2.31 us -> 0.19 us  [spread(): copies = jnp.broadcast_to(value[None], (lax.axis_size(axes),) + value.shape)]
  transfers between devices with their start and end apart: 3 -> 3, of which waited for: 3 -> 3; matrix products, arithmetic and copies ran while one was open for 2% -> 1% of each run, Pallas kernels for 0% -> 0%
where the time goes in v2:
time: 189 us; the launch traced here: 188 us
  blocking collectives  100 us (53%)
  starting transfers between devices  40 us (21%)
  local copies, waits for them, and re-layouts  14.8 us (8%)
  waiting for transfers between devices  14.4 us (8%)
  other arithmetic  9.68 us (5%)
  matrix products  7.73 us (4%)
    all_to_all x6, blocking collectives, exchange(): return lax.all_to_all(pieces, axes, split_axis=0, concat_axis=0, tiled=True)  100 us
    all_to_all x1, starting transfers between devices, exchange(): return lax.all_to_all(pieces, axes, split_axis=0, concat_axis=0, tiled=True)  20.1 us
    ppermute x1, starting transfers between devices, on_device(): far = lax.ppermute(near, 'zh', [(0, 1), (1, 0)])  11.7 us
    all_to_all x1, waiting for transfers between devices, exchange(): return lax.all_to_all(pieces, axes, split_axis=0, concat_axis=0, tiled=True)  10.9 us
    ppermute x1, starting transfers between devices, on_device(): other_core = lax.ppermute(same_core, 'c', [(0, 1), (1, 0)])  8.23 us
    unnamed x9, local copies, waits for them, and re-layouts  3.88 us
  transfers between devices with their start and end apart: 3, of which 3 were waited for; matrix products, arithmetic and copies ran while one was open for 1% of the time, Pallas kernels for 0%

profile of v2, /device:TPU:1, one launch (start us, length us, event | category | flops | bytes accessed | tf_op | source)
XLA Modules:
  0.0 188.1 jit_solution(12776847832639370045)
XLA Ops:
  0.6 0.0 copy-start
  0.7 1.6 slice.7
  2.2 1.5 reshape.157
  3.7 0.9 dynamic-slice_reduce_fusion
  4.6 1.6 fusion.1
  6.2 0.6 broadcast.193
  6.8 2.3 %reduce.5 = bf16[96,512]{1,0:T(8,128)(2,1)} reduce(bf16[96,1,512]{2,0,1:T(8,128)(2,1)} %fusion.1, bf16[]{:T(256)} %broadcast.193), dimensions={1}, to_apply=%copy.11.reduce_sub_computation | reduce | bytes 196610 | tf_op jit(solution)/shard_map/all_to_all | solution.py:14
  9.1 1.6 reshape.172
  10.6 20.1 %all-to-all-start = ((bf16[96,2,256]{2,1,0:T(2,128)(2,1)}), bf16[96,2,256]{2,1,0:T(2,128)(2,1)}, u32[]{:S(2)}, u32[]{:S(2)}) async-start(bf16[96,2,256]{2,1,0:T(2,128)(2,1)} %reshape.172), calls=%async_computation | async-start | bytes 196608 | tf_op jit(solution)/shard_map/all_to_all | solution.py:14
  30.8 0.0 copy-start.1
  30.8 1.6 slice.6
  32.4 0.8 compare_reduce_fusion
  33.1 0.1 convert_reduce_fusion
  33.2 10.9 %all-to-all-done = bf16[96,2,256]{2,1,0:T(2,128)(2,1)} async-done(((bf16[96,2,256]{2,1,0:T(2,128)(2,1)}), bf16[96,2,256]{2,1,0:T(2,128)(2,1)}, u32[]{:S(2)}, u32[]{:S(2)}) %all-to-all-start) | async-done | bytes 98336 | tf_op jit(solution)/shard_map/all_to_all | solution.py:14
  44.2 1.6 reshape.173
  45.8 1.7 convolution_convert_fusion.1
  47.5 1.5 reshape.158
  49.0 0.8 fusion.13
  49.7 0.2 broadcast_in_dim.39
  49.9 39.2 %all_to_all.47 = bf16[48,96,128]{2,1,0:T(8,128)(2,1)S(1)} all-to-all(bf16[48,96,128]{2,1,0:T(8,128)(2,1)S(1)} %broadcast_in_dim.39), channel_id=1, replica_groups=mesh['zh'=2,'x'=4,'y'=8,'zl'=6,'c'=2] {'y','zl'}, dimensions={0} | all-to-all | bytes 2359296 | tf_op jit(solution)/shard_map/all_to_all | solution.py:14
  89.1 8.2 %collective-permute-start = (bf16[48,96,128]{2,1,0:T(8,128)(2,1)S(1)}, bf16[48,96,128]{2,1,0:T(8,128)(2,1)S(1)}, u32[]{:S(2)}, u32[]{:S(2)}) collective-permute-start(bf16[48,96,128]{2,1,0:T(8,128)(2,1)S(1)} %all_to_all.47), channel_id=1, source_target_pairs={{0,1},{1,0},{2,3},{3,2},{4,5},{5,4},{6,7},{7,6},{8,9},{9,8},{10,11... | collective-permute-start | bytes 3538952 | tf_op jit(solution)/shard_map/ppermute | solution.py:56
  98.0 0.0 copy-done.1
  98.0 1.7 collective-permute-done
  99.8 1.6 pad_maximum_fusion
  101.4 3.1 %gather_fusion = bf16[24,96,128]{2,1,0:T(8,128)(2,1)} fusion(bf16[96,96,128]{2,1,0:T(8,128)(2,1)} %pad_maximum_fusion, s32[1024]{0:T(1024)S(1)} %pad_clamp_fusion), kind=kCustom, calls=%fused_computation | custom fusion | bytes 1179744 | tf_op jit(solution)/shard_map/jit(_take)/gather | solution.py:61
  104.5 0.0 copy-done
  104.5 2.0 %fusion = bf16[128,768]{1,0:T(8,128)(2,1)S(1)} fusion(bf16[24,96,768]{2,1,0:T(8,128)(2,1)S(1)} %copy-done, bf16[24,96,128]{2,1,0:T(8,128)(2,1)} %gather_fusion, pred[24]{0:T(512)(128)(4,1)S(1)} %get-tuple-element.4, pred[24]{0:T(512)(128)(4,1)S(1)} %get-tuple-element.5), kind=kOutput, calls=%fused_computation.3 | convolution fusion | flops 453672960 | bytes 4325424 | tf_op jit(solution)/shard_map/dot_general | solution.py:64
  106.5 9.2 %all_to_all.48 = bf16[4,32,768]{2,1,0:T(8,128)(2,1)} all-to-all(bf16[4,32,768]{2,1,0:T(8,128)(2,1)S(1)} %bitcast.55), channel_id=1, replica_groups=mesh['zh'=2,'x'=4,'y'=8,'zl'=6,'c'=2] {'x'}, dimensions={0} | all-to-all | bytes 393216 | tf_op jit(solution)/shard_map/all_to_all | solution.py:14
  115.7 1.6 reduce_sum.40
  117.3 0.0 copy-start.2
  117.3 11.7 %collective-permute-start.1 = (bf16[32,768]{1,0:T(8,128)(2,1)}, bf16[32,768]{1,0:T(8,128)(2,1)S(1)}, u32[]{:S(2)}, u32[]{:S(2)}) collective-permute-start(bf16[32,768]{1,0:T(8,128)(2,1)} %reduce_sum.40), channel_id=1, source_target_pairs={{0,384},{384,0},{1,385},{385,1},{2,386},{386,2},{3,387},{387,3},{4... | collective-permute-start | bytes 147464 | tf_op jit(solution)/shard_map/ppermute | solution.py:69
  129.0 1.7 collective-permute-done.1
  130.7 0.8 add_convert_fusion
  131.6 7.5 %all_to_all.49 = bf16[4,32,768]{2,1,0:T(8,128)(2,1)S(1)} all-to-all(bf16[4,32,768]{2,1,0:T(8,128)(2,1)S(1)} %broadcast_in_dim.69), channel_id=1, replica_groups=mesh['zh'=2,'x'=4,'y'=8,'zl'=6,'c'=2] {'x'}, dimensions={0} | all-to-all | bytes 393216 | tf_op jit(solution)/shard_map/all_to_all | solution.py:14
  139.1 2.0 %multiply_convert_fusion.1 = (bf16[768,256]{1,0:T(8,128)(2,1)}, f32[768,256]{1,0:T(8,128)S(1)}) fusion(bf16[128,768]{1,0:T(8,128)(2,1)S(1)} %bitcast.57, bf16[128,256]{1,0:T(8,128)(2,1)} %param.13), kind=kOutput, calls=%fused_computation.8 | convolution fusion | flops 51314688 | bytes 1441792 | tf_op jit(solution)/shard_map/dot_general | solution.py:73
  141.1 0.0 copy-done.2
  141.1 0.5 fusion.6
  141.5 16.8 %all_to_all.50 = f32[16,8,256]{2,1,0:T(8,128)} all-to-all(f32[16,8,256]{2,1,0:T(8,128)S(1)} %fusion.6), channel_id=1, replica_groups=mesh['zh'=2,'x'=4,'y'=8,'zl'=6,'c'=2] {'y','c'}, dimensions={0} | all-to-all | bytes 262144 | tf_op jit(solution)/shard_map/all_to_all | solution.py:14
  158.3 0.9 reduce_sum.41
  159.2 14.4 %all_to_all.51 = f32[6,8,256]{2,1,0:T(8,128)} all-to-all(f32[6,8,256]{2,1,0:T(8,128)S(1)} %broadcast_in_dim.70), channel_id=1, replica_groups=mesh['zh'=2,'x'=4,'y'=8,'zl'=6,'c'=2] {'zl'}, dimensions={0} | all-to-all | bytes 98304 | tf_op jit(solution)/shard_map/all_to_all | solution.py:14
  173.6 0.8 reduce_sum.42
  174.4 13.0 %all_to_all.52 = f32[16,8,256]{2,1,0:T(8,128)S(1)} all-to-all(f32[16,8,256]{2,1,0:T(8,128)S(1)} %broadcast_in_dim.71), channel_id=1, replica_groups=mesh['zh'=2,'x'=4,'y'=8,'zl'=6,'c'=2] {'y','c'}, dimensions={0} | all-to-all | bytes 262144 | tf_op jit(solution)/shard_map/all_to_all | solution.py:14
  187.5 0.7 copy.20
  (6 shorter events, 0.1 us)
Async XLA Ops:
  0.6 103.9 %copy-start = (bf16[24,96,768]{2,1,0:T(8,128)(2,1)S(1)}, bf16[24,96,768]{2,1,0:T(8,128)(2,1)}, u32[]{:S(2)}) copy-start(bf16[24,96,768]{2,1,0:T(8,128)(2,1)} %param.9) | copy-start | bytes 10616836
  10.6 33.5 %all-to-all-start = ((bf16[96,2,256]{2,1,0:T(2,128)(2,1)}), bf16[96,2,256]{2,1,0:T(2,128)(2,1)}, u32[]{:S(2)}, u32[]{:S(2)}) async-start(bf16[96,2,256]{2,1,0:T(2,128)(2,1)} %reshape.172), calls=%async_computation | async-start | bytes 196608 | tf_op jit(solution)/shard_map/all_to_all | solution.py:14
  30.8 67.2 %copy-start.1 = (s32[1,24]{1,0:T(1,128)S(1)}, s32[1,24]{1,0:T(1,128)}, u32[]{:S(2)}) copy-start(s32[1,24]{1,0:T(1,128)} %param.10) | copy-start | bytes 292
  89.1 10.7 %collective-permute-start = (bf16[48,96,128]{2,1,0:T(8,128)(2,1)S(1)}, bf16[48,96,128]{2,1,0:T(8,128)(2,1)S(1)}, u32[]{:S(2)}, u32[]{:S(2)}) collective-permute-start(bf16[48,96,128]{2,1,0:T(8,128)(2,1)S(1)} %all_to_all.47), channel_id=1, source_target_pairs={{0,1},{1,0},{2,3},{3,2},{4,5},{5,4},{6,7},{7,6},{8,9},{9,8},{10,11... | collective-permute-start | bytes 3538952 | tf_op jit(solution)/shard_map/ppermute | solution.py:56
  117.3 23.8 %copy-start.2 = (bf16[768,256]{1,0:T(8,128)(2,1)S(1)}, bf16[768,256]{1,0:T(8,128)(2,1)}, u32[]{:S(2)}) copy-start(bf16[768,256]{1,0:T(8,128)(2,1)} %param.12) | copy-start | bytes 1179652
  117.3 13.4 %collective-permute-start.1 = (bf16[32,768]{1,0:T(8,128)(2,1)}, bf16[32,768]{1,0:T(8,128)(2,1)S(1)}, u32[]{:S(2)}, u32[]{:S(2)}) collective-permute-start(bf16[32,768]{1,0:T(8,128)(2,1)} %reduce_sum.40), channel_id=1, source_target_pairs={{0,384},{384,0},{1,385},{385,1},{2,386},{386,2},{3,387},{387,3},{4... | collective-permute-start | bytes 147464 | tf_op jit(solution)/shard_map/ppermute | solution.py:69

commit v3 on v2

v3 whole, which is shorter than its diff:
```python
import functools

import jax
import jax.numpy as jnp
from jax import lax
from jax.experimental import pallas as pl
from jax.experimental.pallas import tpu as pltpu
from jax.sharding import Mesh, PartitionSpec as P

KEEP = 576
GRP = ("zh", "x")
ROW = ("y", "zl", "c")
FINE = (2, 4, 8, 6, 2)


def exchange(pieces, axes):
    return lax.all_to_all(pieces, axes, split_axis=0, concat_axis=0, tiled=True)


def spread(value, axes):
    copies = jnp.broadcast_to(value[None], (lax.axis_size(axes),) + value.shape)
    return exchange(copies, axes)


def vmem():
    return pl.BlockSpec(memory_space=pltpu.VMEM)


def smem():
    return pl.BlockSpec(memory_space=pltpu.SMEM)


def contract_last(first, second):
    return lax.dot_general(
        first, second, (((1,), (1,)), ((), ())), preferred_element_type=jnp.float32
    )


def grid_of(shape, axis):
    return lax.broadcasted_iota(jnp.int32, shape, axis)


def places_kernel(first_moving, held, role_ref, slot_ref, plan_ref, column_ref, mine_ref, theirs_ref, sent_ref):
    row_count, leaving = plan_ref.shape
    slot_count = column_ref.shape[1]
    half_rows = row_count // 2
    group, core, live = role_ref[0], role_ref[1], role_ref[2]
    half = jnp.maximum(group - first_moving, 0)

    eye = (grid_of((leaving, leaving), 0) == grid_of((leaving, leaving), 1)).astype(jnp.float32)
    plan = contract_last(eye.astype(jnp.bfloat16), plan_ref[...].astype(jnp.float32).astype(jnp.bfloat16))
    plan = plan.astype(jnp.int32)
    numbers = grid_of(plan.shape, 0) + 1
    for slot in range(slot_count):
        hits = jnp.where(plan == slot_ref[0, slot], numbers, 0)
        sent_ref[slot : slot + 1, :] = jnp.sum(hits.astype(jnp.float32), axis=0, keepdims=True)
    sent = sent_ref[...]

    square = (row_count, row_count)
    before = (grid_of(square, 1) < grid_of(square, 0)).astype(jnp.float32).astype(jnp.bfloat16)
    same = (grid_of(square, 1) == grid_of(square, 0)).astype(jnp.float32).astype(jnp.bfloat16)
    flags = jnp.where(sent > 0, 1.0, 0.0).astype(jnp.bfloat16)
    ranks = contract_last(before, flags).astype(jnp.int32)
    numbers = contract_last(same, sent.astype(jnp.bfloat16)).astype(jnp.int32) - 1

    source = grid_of(numbers.shape, 0)
    offset = (source >> 1) * held + jnp.where((source & 1) == core, 0, half_rows * held)
    local = numbers - half * held
    here = (numbers >= 0) & (local >= 0) & (local < held)
    none_held = row_count * held
    words = jnp.where(here, offset + local - none_held, 0)
    ranks = jnp.where(numbers >= 0, ranks, -1)

    columns = column_ref[...]
    column_base = (columns >> 1) * held + jnp.where((columns & 1) == core, 0, half_rows * held)
    dead = grid_of(columns.shape, 1) >= live
    for order in range(held):
        chosen = jnp.where(ranks == half * held + order, words, 0)
        moved = none_held + jnp.sum(chosen, axis=0, keepdims=True)
        stayed = column_base + order
        own = jnp.where(group >= first_moving, moved, stayed)
        mine_ref[order : order + 1, :] = jnp.where(dead, none_held, own)
        chosen = jnp.where(ranks == (1 - half) * held + order, words, 0)
        other = none_held + jnp.sum(chosen, axis=0, keepdims=True)
        theirs_ref[order : order + 1, :] = jnp.where(dead, none_held, other)


def part_places(role, columns, dest_plan, first_moving, held):
    shape = jax.ShapeDtypeStruct((held, columns.shape[1]), jnp.int32)
    return pl.pallas_call(
        functools.partial(places_kernel, first_moving, held),
        out_shape=(shape, shape),
        in_specs=[smem(), smem(), vmem(), vmem()],
        out_specs=(vmem(), vmem()),
        scratch_shapes=[pltpu.VMEM((columns.shape[1], dest_plan.shape[0]), jnp.float32)],
        cost_estimate=pl.CostEstimate(flops=4000000, bytes_accessed=50000, transcendentals=0),
    )(role, columns, dest_plan, columns)


def pick_kernel(place_ref, first_ref, second_ref, out_ref, held_ref, sems):
    half = first_ref.shape[0]
    first = pltpu.make_async_copy(first_ref, held_ref.at[pl.ds(0, half)], sems.at[0])
    second = pltpu.make_async_copy(second_ref, held_ref.at[pl.ds(half, half)], sems.at[1])
    first.start()
    second.start()
    held_ref[2 * half] = jnp.zeros(held_ref.shape[1:], held_ref.dtype)
    first.wait()
    second.wait()
    orders, slots = place_ref.shape

    def one_slot(slot, carry):
        for order in range(orders):
            out_ref[slot * orders + order] = held_ref[place_ref[order, slot]]
        return carry

    lax.fori_loop(0, slots, one_slot, 0)


def pick_parts(places, first, second):
    part = first.shape[1:]
    count = places.shape[0] * places.shape[1]
    return pl.pallas_call(
        pick_kernel,
        out_shape=jax.ShapeDtypeStruct((count,) + part, first.dtype),
        in_specs=[smem()] + [pl.BlockSpec(memory_space=pl.ANY)] * 2,
        out_specs=vmem(),
        scratch_shapes=[
            pltpu.VMEM((2 * first.shape[0] + 8,) + part, first.dtype),
            pltpu.SemaphoreType.DMA((2,)),
        ],
        compiler_params=pltpu.CompilerParams(vmem_limit_bytes=32 * 1024 * 1024),
        cost_estimate=pl.CostEstimate(flops=1000000, bytes_accessed=3000000, transcendentals=0),
    )(places, first, second)


def on_device(features, dest_plan, adj_tiles, tile_cols, tile_count, grad_out, weight):
    block_rows, feat_width = features.shape
    hid = weight.shape[1]
    own_group = lax.axis_index(GRP)
    leaving = dest_plan.shape[1]
    part_rows = (block_rows - KEEP) // leaving
    slice_rows = block_rows // lax.axis_size(GRP)
    held = slice_rows // part_rows
    first_moving = KEEP // slice_rows
    part_shape = (-1, part_rows, feat_width)

    own_slice = lax.dynamic_slice_in_dim(features, own_group * slice_rows, slice_rows, 0)
    same_core = spread(spread(own_slice, "zl"), "y").reshape(part_shape)
    other_core = lax.ppermute(same_core, "c", [(0, 1), (1, 0)])
    role = jnp.stack([own_group, lax.axis_index("c"), tile_count[0]])
    mine, theirs = part_places(role, tile_cols, dest_plan, first_moving, held)
    for_peer = pick_parts(theirs, same_core, other_core)
    from_peer = lax.ppermute(
        for_peer, GRP, [(first_moving, first_moving + 1), (first_moving + 1, first_moving)]
    )
    picked = pick_parts(mine, same_core, other_core) + from_peer
    picked = picked.reshape(adj_tiles.shape[0], slice_rows, feat_width)

    partial_value = lax.dot_general(
        picked, adj_tiles, (((0, 1), (0, 1)), ((), ())), preferred_element_type=jnp.float32
    ).astype(jnp.bfloat16)
    terms = exchange(partial_value, "x").reshape(lax.axis_size("x"), -1, block_rows)
    near = jnp.sum(terms.astype(jnp.float32), axis=0).astype(jnp.bfloat16)
    far = lax.ppermute(near, "zh", [(0, 1), (1, 0)])
    own_feats = (near.astype(jnp.float32) + far.astype(jnp.float32)).astype(jnp.bfloat16)
    aggregated = spread(own_feats, "x").reshape(feat_width, block_rows)

    projected = lax.dot_general(
        aggregated, weight, (((0,), (0,)), ((), ())), preferred_element_type=jnp.float32
    )
    sigmoid_part = jax.nn.sigmoid(projected)
    activated = (projected * sigmoid_part).astype(jnp.bfloat16)
    slope = sigmoid_part * (1.0 + projected * (1.0 - sigmoid_part))
    masked = (grad_out.astype(jnp.float32) * slope).astype(jnp.bfloat16)
    local_grad = jnp.dot(aggregated, masked, preferred_element_type=jnp.float32)

    ring_terms = exchange(local_grad, ("y", "c")).reshape(lax.axis_size(("y", "c")), -1, hid)
    line_terms = spread(jnp.sum(ring_terms, axis=0), "zl")
    own_grad = jnp.sum(line_terms.reshape((-1,) + ring_terms.shape[1:]), axis=0)
    weight_grad = spread(own_grad, ("y", "c")).reshape(feat_width, hid)
    return (activated, weight_grad)


def solution(mesh):
    fine_mesh = Mesh(mesh.devices.reshape(FINE), GRP + ROW)
    in_specs = (
        P(ROW, None),
        P(),
        P(None, GRP, ROW),
        P(ROW, None),
        P(ROW),
        P(ROW, None),
        P(),
    )
    out_specs = (P(ROW, None), P())
    return jax.shard_map(
        on_device, mesh=fine_mesh, in_specs=in_specs, out_specs=out_specs, check_vma=False
    )
```

time: 189 us -> 169 us (0.89)
  blocking collectives: 100 us -> 114 us
  waiting for transfers between devices: 14.4 us -> 1.68 us
  starting transfers between devices: 40 us -> 29 us
  local copies, waits for them, and re-layouts: 14.8 us -> 4.67 us
  Pallas kernels: 0 us -> 8.64 us
  matrix products: 7.73 us -> 3.14 us
  other arithmetic: 9.68 us -> 5.11 us
    all_to_all x1 -> x0, starting transfers between devices: 20.1 us -> none  [exchange(): return lax.all_to_all(pieces, axes, split_axis=0, concat_axis=0, tiled=True)]
    all_to_all x6 -> x7, blocking collectives: 100 us -> 114 us  [exchange(): return lax.all_to_all(pieces, axes, split_axis=0, concat_axis=0, tiled=True)]
    all_to_all x1 -> x0, waiting for transfers between devices: 10.9 us -> none  [exchange(): return lax.all_to_all(pieces, axes, split_axis=0, concat_axis=0, tiled=True)]
    ppermute x1, starting transfers between devices: 11.7 us -> 21.8 us  [on_device(): far = lax.ppermute(near, 'zh', [(0, 1), (1, 0)])]
    pallas_call x0 -> x3, Pallas kernels: none -> 8.64 us  [the longest x2 6.45 us: pick_parts(): pl.pallas_call(pick_kernel, out_shape=jax.ShapeDtypeStruct((count,) + par...]
    dot_general x2 -> x0, matrix products: 3.29 us -> none  [the longest x1 1.69 us: relocate(): jnp.dot(chooser, arrived, preferred_element_type=jnp.float32)]
    slice x2 -> x0, local copies, waits for them, and re-layouts: 3.15 us -> none  [the longest x1 1.58 us: relocate(): features[:KEEP]]
    gather x1 -> x0, local copies, waits for them, and re-layouts: 3.13 us -> none  [on_device(): picked = jnp.take(gathered, places, axis=0)]
  transfers between devices with their start and end apart: 3 -> 3, of which waited for: 3 -> 1; matrix products, arithmetic and copies ran while one was open for 1% -> 1% of each run, Pallas kernels for 0% -> 3%
where the time goes in v3:
time: 169 us; the launch traced here: 168 us
  blocking collectives  114 us (67%)
  starting transfers between devices  29 us (17%)
  Pallas kernels  8.64 us (5%)
  other arithmetic  5.11 us (3%)
  local copies, waits for them, and re-layouts  4.67 us (3%)
  matrix products  3.14 us (2%)
    all_to_all x7, blocking collectives, exchange(): return lax.all_to_all(pieces, axes, split_axis=0, concat_axis=0, tiled=True)  114 us
    ppermute x1, starting transfers between devices, on_device(): far = lax.ppermute(near, 'zh', [(0, 1), (1, 0)])  21.8 us
    ppermute x1, starting transfers between devices, on_device(): other_core = lax.ppermute(same_core, 'c', [(0, 1), (1, 0)])  6.54 us
    pallas_call x2, Pallas kernels, pick_parts(): pl.pallas_call(pick_kernel, out_shape=jax.ShapeDtypeStruct((count,) + par...  6.45 us
    unnamed x10, local copies, waits for them, and re-layouts  3.53 us
  transfers between devices with their start and end apart: 3, of which 1 were waited for; matrix products, arithmetic and copies ran while one was open for 1% of the time, Pallas kernels for 3%

profile of v3, /device:TPU:1, one launch (start us, length us, event | category | flops | bytes accessed | tf_op | source)
XLA Modules:
  0.0 167.7 jit_solution(7538767890800023789)
XLA Ops:
  0.6 0.0 copy-start
  0.7 0.9 constant_dynamic-slice_fusion
  1.6 20.9 %all_to_all.40 = bf16[6,96,128]{2,1,0:T(8,128)(2,1)S(1)} all-to-all(bf16[6,96,128]{2,1,0:T(8,128)(2,1)S(1)} %broadcast_in_dim.10), channel_id=1, replica_groups=mesh['zh'=2,'x'=4,'y'=8,'zl'=6,'c'=2] {'zl'}, dimensions={0} | all-to-all | bytes 294912 | tf_op jit(solution)/shard_map/all_to_all | solution.py:17
  22.5 0.2 broadcast_in_dim.11
  22.7 34.6 %all_to_all.41 = bf16[8,6,96,128]{3,2,1,0:T(8,128)(2,1)} all-to-all(bf16[8,6,96,128]{3,2,1,0:T(8,128)(2,1)S(1)} %broadcast_in_dim.11), channel_id=1, replica_groups=mesh['zh'=2,'x'=4,'y'=8,'zl'=6,'c'=2] {'y'}, dimensions={0} | all-to-all | bytes 2359296 | tf_op jit(solution)/shard_map/all_to_all | solution.py:17
  57.3 6.5 %collective-permute-start = (bf16[1152,4,128]{2,1,0:T(4,128)(2,1)}, bf16[1152,4,128]{2,1,0:T(4,128)(2,1)}, u32[]{:S(2)}, u32[]{:S(2)}) collective-permute-start(bf16[1152,4,128]{2,1,0:T(4,128)(2,1)} %bitcast.2.first_ref), channel_id=1, source_target_pairs={{0,1},{1,0},{2,3},{3,2},{4,5},{5,4},{6,7},{7,6},{8,9},{9,8},{10,11... | collective-permute-start | bytes 3538952 | tf_op jit(solution)/shard_map/ppermute | solution.py:149
  64.5 1.5 copy.10.plan_ref
  65.9 0.7 pad_add_fusion.role_ref
  66.6 2.2 %shard_map.86 = (s32[24,24]{1,0:T(8,128)}, s32[24,24]{1,0:T(8,128)}) custom-call(s32[3]{0:T(128)} %pad_add_fusion.role_ref, s32[1,24]{1,0:T(1,128)} %column_ref.1, s32[96,48]{1,0:T(8,128)} %copy.10.plan_ref, s32[1,24]{1,0:T(1,128)} %column_ref.1), custom_call_target="tpu_custom_call" | custom-call | flops 4000000 | bytes 50000 | tf_op jit(solution)/shard_map/pallas_call | solution.py:90
  68.8 0.0 collective-permute-done.second_ref
  68.8 0.0 copy-start.2
  68.8 0.7 copy-done.2
  69.5 3.2 %shard_map.88 = bf16[576,4,128]{2,1,0:T(4,128)(2,1)S(1)} custom-call(s32[24,24]{1,0:T(8,128)S(1)} %copy-done.2, bf16[1152,4,128]{2,1,0:T(4,128)(2,1)} %bitcast.2.first_ref, bf16[1152,4,128]{2,1,0:T(4,128)(2,1)} %collective-permute-done.second_ref), custom_call_target="tpu_custom_call" | custom-call | flops 1000000 | bytes 3000000 | tf_op jit(solution)/shard_map/pallas_call | solution.py:122
  72.7 0.7 collective-permute-start.1
  73.4 0.0 copy-start.1
  73.5 0.7 copy-done.1
  74.2 3.2 %shard_map.87 = bf16[576,4,128]{2,1,0:T(4,128)(2,1)S(1)} custom-call(s32[24,24]{1,0:T(8,128)S(1)} %copy-done.1, bf16[1152,4,128]{2,1,0:T(4,128)(2,1)} %bitcast.2.first_ref, bf16[1152,4,128]{2,1,0:T(4,128)(2,1)} %collective-permute-done.second_ref), custom_call_target="tpu_custom_call" | custom-call | flops 1000000 | bytes 3000000 | tf_op jit(solution)/shard_map/pallas_call | solution.py:122
  77.4 0.0 collective-permute-done.1
  77.4 0.3 add.20
  77.7 0.0 copy-done
  77.7 0.7 fusion
  78.4 9.4 %all_to_all.42 = bf16[4,32,768]{2,1,0:T(8,128)(2,1)} all-to-all(bf16[4,32,768]{2,1,0:T(8,128)(2,1)S(1)} %bitcast.21), channel_id=1, replica_groups=mesh['zh'=2,'x'=4,'y'=8,'zl'=6,'c'=2] {'x'}, dimensions={0} | all-to-all | bytes 393216 | tf_op jit(solution)/shard_map/all_to_all | solution.py:17
  87.8 1.6 reduce_sum.30
  89.4 0.0 copy-start.3
  89.4 21.8 %collective-permute-start.2 = (bf16[32,768]{1,0:T(8,128)(2,1)}, bf16[32,768]{1,0:T(8,128)(2,1)S(1)}, u32[]{:S(2)}, u32[]{:S(2)}) collective-permute-start(bf16[32,768]{1,0:T(8,128)(2,1)} %reduce_sum.30), channel_id=1, source_target_pairs={{0,384},{384,0},{1,385},{385,1},{2,386},{386,2},{3,387},{387,3},{4... | collective-permute-start | bytes 147464 | tf_op jit(solution)/shard_map/ppermute | solution.py:164
  111.2 1.7 %collective-permute-done.2 = bf16[32,768]{1,0:T(8,128)(2,1)S(1)} collective-permute-done((bf16[32,768]{1,0:T(8,128)(2,1)}, bf16[32,768]{1,0:T(8,128)(2,1)S(1)}, u32[]{:S(2)}, u32[]{:S(2)}) %collective-permute-start.2) | collective-permute-done | bytes 49184 | tf_op jit(solution)/shard_map/ppermute | solution.py:164
  112.9 0.8 add_convert_fusion
  113.7 7.5 %all_to_all.43 = bf16[4,32,768]{2,1,0:T(8,128)(2,1)S(1)} all-to-all(bf16[4,32,768]{2,1,0:T(8,128)(2,1)S(1)} %broadcast_in_dim.12), channel_id=1, replica_groups=mesh['zh'=2,'x'=4,'y'=8,'zl'=6,'c'=2] {'x'}, dimensions={0} | all-to-all | bytes 393216 | tf_op jit(solution)/shard_map/all_to_all | solution.py:17
  121.3 2.0 %multiply_convert_fusion.1 = (bf16[768,256]{1,0:T(8,128)(2,1)}, f32[768,256]{1,0:T(8,128)S(1)}) fusion(bf16[128,768]{1,0:T(8,128)(2,1)S(1)} %bitcast.23, bf16[128,256]{1,0:T(8,128)(2,1)} %param.13), kind=kOutput, calls=%fused_computation.3 | convolution fusion | flops 51314688 | bytes 1441792 | tf_op jit(solution)/shard_map/dot_general | solution.py:168
  123.3 0.0 copy-done.3
  123.3 0.5 fusion.1
  123.7 16.5 %all_to_all.44 = f32[16,8,256]{2,1,0:T(8,128)} all-to-all(f32[16,8,256]{2,1,0:T(8,128)S(1)} %fusion.1), channel_id=1, replica_groups=mesh['zh'=2,'x'=4,'y'=8,'zl'=6,'c'=2] {'y','c'}, dimensions={0} | all-to-all | bytes 262144 | tf_op jit(solution)/shard_map/all_to_all | solution.py:17
  140.3 0.9 reduce_sum.31
  141.2 12.0 %all_to_all.45 = f32[6,8,256]{2,1,0:T(8,128)} all-to-all(f32[6,8,256]{2,1,0:T(8,128)S(1)} %broadcast_in_dim.13), channel_id=1, replica_groups=mesh['zh'=2,'x'=4,'y'=8,'zl'=6,'c'=2] {'zl'}, dimensions={0} | all-to-all | bytes 98304 | tf_op jit(solution)/shard_map/all_to_all | solution.py:17
  153.2 0.8 reduce_sum.32
  154.0 13.0 %all_to_all.46 = f32[16,8,256]{2,1,0:T(8,128)S(1)} all-to-all(f32[16,8,256]{2,1,0:T(8,128)S(1)} %broadcast_in_dim.14), channel_id=1, replica_groups=mesh['zh'=2,'x'=4,'y'=8,'zl'=6,'c'=2] {'y','c'}, dimensions={0} | all-to-all | bytes 262144 | tf_op jit(solution)/shard_map/all_to_all | solution.py:17
  167.0 0.7 copy.13
  (4 shorter events, 0.1 us)
Async XLA Ops:
  0.6 77.1 %copy-start = (bf16[24,96,768]{2,1,0:T(8,128)(2,1)S(1)}, bf16[24,96,768]{2,1,0:T(8,128)(2,1)}, u32[]{:S(2)}) copy-start(bf16[24,96,768]{2,1,0:T(8,128)(2,1)} %param.9) | copy-start | bytes 10616836
  57.3 11.5 %collective-permute-start = (bf16[1152,4,128]{2,1,0:T(4,128)(2,1)}, bf16[1152,4,128]{2,1,0:T(4,128)(2,1)}, u32[]{:S(2)}, u32[]{:S(2)}) collective-permute-start(bf16[1152,4,128]{2,1,0:T(4,128)(2,1)} %bitcast.2.first_ref), channel_id=1, source_target_pairs={{0,1},{1,0},{2,3},{3,2},{4,5},{5,4},{6,7},{7,6},{8,9},{9,8},{10,11... | collective-permute-start | bytes 3538952 | tf_op jit(solution)/shard_map/ppermute | solution.py:149
  68.8 0.7 copy-start.2
  72.7 4.7 %collective-permute-start.1 = (bf16[576,4,128]{2,1,0:T(4,128)(2,1)S(1)}, bf16[576,4,128]{2,1,0:T(4,128)(2,1)S(1)}, u32[]{:S(2)}, u32[]{:S(2)}) collective-permute-start(bf16[576,4,128]{2,1,0:T(4,128)(2,1)S(1)} %shard_map.88), channel_id=1, source_target_pairs={{576,672},{672,576},{577,673},{673,577},{578,674},{674,578},{579,6... | collective-permute-start | bytes 1769480 | tf_op jit(solution)/shard_map/ppermute | solution.py:153
  73.4 0.7 copy-start.1
  89.4 33.8 %copy-start.3 = (bf16[768,256]{1,0:T(8,128)(2,1)S(1)}, bf16[768,256]{1,0:T(8,128)(2,1)}, u32[]{:S(2)}) copy-start(bf16[768,256]{1,0:T(8,128)(2,1)} %param.12) | copy-start | bytes 1179652
  89.4 23.5 %collective-permute-start.2 = (bf16[32,768]{1,0:T(8,128)(2,1)}, bf16[32,768]{1,0:T(8,128)(2,1)S(1)}, u32[]{:S(2)}, u32[]{:S(2)}) collective-permute-start(bf16[32,768]{1,0:T(8,128)(2,1)} %reduce_sum.30), channel_id=1, source_target_pairs={{0,384},{384,0},{1,385},{385,1},{2,386},{386,2},{3,387},{387,3},{4... | collective-permute-start | bytes 147464 | tf_op jit(solution)/shard_map/ppermute | solution.py:164

commit v4 on v3

--- a/solution.py
+++ b/solution.py
@@ -40,16 +40,16 @@
     return lax.broadcasted_iota(jnp.int32, shape, axis)
 
 
-def places_kernel(first_moving, held, role_ref, slot_ref, plan_ref, column_ref, mine_ref, theirs_ref, sent_ref):
-    row_count, leaving = plan_ref.shape
+def places_kernel(
+    first_moving, held, group_ref, core_ref, live_ref, slot_ref, plan_ref, column_ref, mine_ref, theirs_ref, sent_ref
+):
+    leaving, row_count = plan_ref.shape
     slot_count = column_ref.shape[1]
     half_rows = row_count // 2
-    group, core, live = role_ref[0], role_ref[1], role_ref[2]
+    group, core, live = group_ref[0], core_ref[0], live_ref[0]
     half = jnp.maximum(group - first_moving, 0)
 
-    eye = (grid_of((leaving, leaving), 0) == grid_of((leaving, leaving), 1)).astype(jnp.float32)
-    plan = contract_last(eye.astype(jnp.bfloat16), plan_ref[...].astype(jnp.float32).astype(jnp.bfloat16))
-    plan = plan.astype(jnp.int32)
+    plan = plan_ref[...]
     numbers = grid_of(plan.shape, 0) + 1
     for slot in range(slot_count):
         hits = jnp.where(plan == slot_ref[0, slot], numbers, 0)
@@ -90,11 +90,11 @@
     return pl.pallas_call(
         functools.partial(places_kernel, first_moving, held),
         out_shape=(shape, shape),
-        in_specs=[smem(), smem(), vmem(), vmem()],
+        in_specs=[smem(), smem(), smem(), smem(), vmem(), vmem()],
         out_specs=(vmem(), vmem()),
         scratch_shapes=[pltpu.VMEM((columns.shape[1], dest_plan.shape[0]), jnp.float32)],
         cost_estimate=pl.CostEstimate(flops=4000000, bytes_accessed=50000, transcendentals=0),
-    )(role, columns, dest_plan, columns)
+    )(*role, columns, dest_plan.T, columns)
 
 
 def pick_kernel(place_ref, first_ref, second_ref, out_ref, held_ref, sems):
@@ -128,7 +128,7 @@
             pltpu.VMEM((2 * first.shape[0] + 8,) + part, first.dtype),
             pltpu.SemaphoreType.DMA((2,)),
         ],
-        compiler_params=pltpu.CompilerParams(vmem_limit_bytes=32 * 1024 * 1024),
+        compiler_params=pltpu.CompilerParams(vmem_limit_bytes=8 * 1024 * 1024),
         cost_estimate=pl.CostEstimate(flops=1000000, bytes_accessed=3000000, transcendentals=0),
     )(places, first, second)
 
@@ -146,9 +146,9 @@
 
     own_slice = lax.dynamic_slice_in_dim(features, own_group * slice_rows, slice_rows, 0)
     same_core = spread(spread(own_slice, "zl"), "y").reshape(part_shape)
+    role = (own_group.reshape(1), lax.axis_index("c").reshape(1), tile_count)
+    mine, theirs = part_places(role, tile_cols, dest_plan, first_moving, held)
     other_core = lax.ppermute(same_core, "c", [(0, 1), (1, 0)])
-    role = jnp.stack([own_group, lax.axis_index("c"), tile_count[0]])
-    mine, theirs = part_places(role, tile_cols, dest_plan, first_moving, held)
     for_peer = pick_parts(theirs, same_core, other_core)
     from_peer = lax.ppermute(
         for_peer, GRP, [(first_moving, first_moving + 1), (first_moving + 1, first_moving)]

time: 169 us -> 166 us (0.982)
    unnamed x10 -> x9, local copies, waits for them, and re-layouts: 3.53 us -> 2.08 us
  transfers between devices with their start and end apart: 3 -> 3, of which waited for: 1 -> 2; matrix products, arithmetic and copies ran while one was open for 1% -> 0% of each run, Pallas kernels for 3% -> 3%
where the time goes in v4:
time: 166 us; the launch traced here: 165 us
  blocking collectives  114 us (69%)
  starting transfers between devices  28.8 us (17%)
  Pallas kernels  8.43 us (5%)
  other arithmetic  4.44 us (3%)
  local copies, waits for them, and re-layouts  3.22 us (2%)
  matrix products  3.13 us (2%)
  waiting for transfers between devices  1.99 us (1%)
    all_to_all x7, blocking collectives, exchange(): return lax.all_to_all(pieces, axes, split_axis=0, concat_axis=0, tiled=True)  114 us
    ppermute x1, starting transfers between devices, on_device(): far = lax.ppermute(near, 'zh', [(0, 1), (1, 0)])  21.6 us
    ppermute x1, starting transfers between devices, on_device(): other_core = lax.ppermute(same_core, 'c', [(0, 1), (1, 0)])  6.54 us
    pallas_call x2, Pallas kernels, pick_parts(): pl.pallas_call(pick_kernel, out_shape=jax.ShapeDtypeStruct((count,) + par...  6.45 us
  transfers between devices with their start and end apart: 3, of which 2 were waited for; matrix products, arithmetic and copies ran while one was open for 0% of the time, Pallas kernels for 3%

profile of v4, /device:TPU:1, one launch (start us, length us, event | category | flops | bytes accessed | tf_op | source)
XLA Modules:
  0.0 165.5 jit_solution(1486550802763521043)
XLA Ops:
  0.6 0.0 copy-start
  0.7 0.9 constant_dynamic-slice_fusion
  1.6 20.9 %all_to_all.40 = bf16[6,96,128]{2,1,0:T(8,128)(2,1)S(1)} all-to-all(bf16[6,96,128]{2,1,0:T(8,128)(2,1)S(1)} %broadcast_in_dim.10), channel_id=1, replica_groups=mesh['zh'=2,'x'=4,'y'=8,'zl'=6,'c'=2] {'zl'}, dimensions={0} | all-to-all | bytes 294912 | tf_op jit(solution)/shard_map/all_to_all | solution.py:17
  22.5 0.2 broadcast_in_dim.11
  22.7 34.6 %all_to_all.41 = bf16[8,6,96,128]{3,2,1,0:T(8,128)(2,1)} all-to-all(bf16[8,6,96,128]{3,2,1,0:T(8,128)(2,1)S(1)} %broadcast_in_dim.11), channel_id=1, replica_groups=mesh['zh'=2,'x'=4,'y'=8,'zl'=6,'c'=2] {'y'}, dimensions={0} | all-to-all | bytes 2359296 | tf_op jit(solution)/shard_map/all_to_all | solution.py:17
  57.3 6.5 %collective-permute-start = (bf16[1152,4,128]{2,1,0:T(4,128)(2,1)}, bf16[1152,4,128]{2,1,0:T(4,128)(2,1)}, u32[]{:S(2)}, u32[]{:S(2)}) collective-permute-start(bf16[1152,4,128]{2,1,0:T(4,128)(2,1)} %bitcast.3.first_ref), channel_id=1, source_target_pairs={{0,1},{1,0},{2,3},{3,2},{4,5},{5,4},{6,7},{7,6},{8,9},{9,8},{10,11... | collective-permute-start | bytes 3538952 | tf_op jit(solution)/shard_map/ppermute | solution.py:151
  64.5 2.0 %shard_map.86 = (s32[24,24]{1,0:T(8,128)}, s32[24,24]{1,0:T(8,128)}) custom-call(s32[1]{0:T(128)} %bitcast.group_ref, s32[1]{0:T(128)} %bitcast.1.core_ref, s32[1]{0:T(128)S(6)} %copy.10.live_ref, s32[1,24]{1,0:T(1,128)} %column_ref.1, s32[48,96]{1,0:T(8,128)} %bitcast.26, s32[1,24]{1,0:T(1,128)} %column_ref.1), custom_call_target="tpu_custom_call" | custom-call | flops 4000000 | bytes 50000 | tf_op jit(solution)/shard_map/pallas_call | solution.py:90
  66.5 0.2 collective-permute-done.second_ref
  66.6 0.0 copy-start.2
  66.6 0.7 copy-done.2
  67.3 3.2 %shard_map.88 = bf16[576,4,128]{2,1,0:T(4,128)(2,1)S(1)} custom-call(s32[24,24]{1,0:T(8,128)S(1)} %copy-done.2, bf16[1152,4,128]{2,1,0:T(4,128)(2,1)} %bitcast.3.first_ref, bf16[1152,4,128]{2,1,0:T(4,128)(2,1)} %collective-permute-done.second_ref), custom_call_target="tpu_custom_call" | custom-call | flops 1000000 | bytes 3000000 | tf_op jit(solution)/shard_map/pallas_call | solution.py:122
  70.6 0.7 collective-permute-start.1
  71.3 0.0 copy-start.1
  71.3 0.7 copy-done.1
  72.0 3.2 %shard_map.87 = bf16[576,4,128]{2,1,0:T(4,128)(2,1)S(1)} custom-call(s32[24,24]{1,0:T(8,128)S(1)} %copy-done.1, bf16[1152,4,128]{2,1,0:T(4,128)(2,1)} %bitcast.3.first_ref, bf16[1152,4,128]{2,1,0:T(4,128)(2,1)} %collective-permute-done.second_ref), custom_call_target="tpu_custom_call" | custom-call | flops 1000000 | bytes 3000000 | tf_op jit(solution)/shard_map/pallas_call | solution.py:122
  75.2 0.0 collective-permute-done.1
  75.2 0.3 add.20
  75.5 0.0 copy-done
  75.6 0.7 fusion
  76.2 9.2 %all_to_all.42 = bf16[4,32,768]{2,1,0:T(8,128)(2,1)} all-to-all(bf16[4,32,768]{2,1,0:T(8,128)(2,1)S(1)} %bitcast.22), channel_id=1, replica_groups=mesh['zh'=2,'x'=4,'y'=8,'zl'=6,'c'=2] {'x'}, dimensions={0} | all-to-all | bytes 393216 | tf_op jit(solution)/shard_map/all_to_all | solution.py:17
  85.4 1.6 reduce_sum.30
  87.0 0.0 copy-start.3
  87.0 21.6 %collective-permute-start.2 = (bf16[32,768]{1,0:T(8,128)(2,1)}, bf16[32,768]{1,0:T(8,128)(2,1)S(1)}, u32[]{:S(2)}, u32[]{:S(2)}) collective-permute-start(bf16[32,768]{1,0:T(8,128)(2,1)} %reduce_sum.30), channel_id=1, source_target_pairs={{0,384},{384,0},{1,385},{385,1},{2,386},{386,2},{3,387},{387,3},{4... | collective-permute-start | bytes 147464 | tf_op jit(solution)/shard_map/ppermute | solution.py:164
  108.6 1.8 %collective-permute-done.2 = bf16[32,768]{1,0:T(8,128)(2,1)S(1)} collective-permute-done((bf16[32,768]{1,0:T(8,128)(2,1)}, bf16[32,768]{1,0:T(8,128)(2,1)S(1)}, u32[]{:S(2)}, u32[]{:S(2)}) %collective-permute-start.2) | collective-permute-done | bytes 49184 | tf_op jit(solution)/shard_map/ppermute | solution.py:164
  110.5 0.8 add_convert_fusion
  111.3 7.5 %all_to_all.43 = bf16[4,32,768]{2,1,0:T(8,128)(2,1)S(1)} all-to-all(bf16[4,32,768]{2,1,0:T(8,128)(2,1)S(1)} %broadcast_in_dim.12), channel_id=1, replica_groups=mesh['zh'=2,'x'=4,'y'=8,'zl'=6,'c'=2] {'x'}, dimensions={0} | all-to-all | bytes 393216 | tf_op jit(solution)/shard_map/all_to_all | solution.py:17
  118.9 2.0 %multiply_convert_fusion.1 = (bf16[768,256]{1,0:T(8,128)(2,1)}, f32[768,256]{1,0:T(8,128)S(1)}) fusion(bf16[128,768]{1,0:T(8,128)(2,1)S(1)} %bitcast.24, bf16[128,256]{1,0:T(8,128)(2,1)} %param.13), kind=kOutput, calls=%fused_computation.3 | convolution fusion | flops 51314688 | bytes 1441792 | tf_op jit(solution)/shard_map/dot_general | solution.py:168
  120.8 0.0 copy-done.3
  120.8 0.5 fusion.1
  121.3 16.8 %all_to_all.44 = f32[16,8,256]{2,1,0:T(8,128)} all-to-all(f32[16,8,256]{2,1,0:T(8,128)S(1)} %fusion.1), channel_id=1, replica_groups=mesh['zh'=2,'x'=4,'y'=8,'zl'=6,'c'=2] {'y','c'}, dimensions={0} | all-to-all | bytes 262144 | tf_op jit(solution)/shard_map/all_to_all | solution.py:17
  138.1 0.9 reduce_sum.31
  139.0 12.0 %all_to_all.45 = f32[6,8,256]{2,1,0:T(8,128)} all-to-all(f32[6,8,256]{2,1,0:T(8,128)S(1)} %broadcast_in_dim.13), channel_id=1, replica_groups=mesh['zh'=2,'x'=4,'y'=8,'zl'=6,'c'=2] {'zl'}, dimensions={0} | all-to-all | bytes 98304 | tf_op jit(solution)/shard_map/all_to_all | solution.py:17
  151.0 0.8 reduce_sum.32
  151.8 13.0 %all_to_all.46 = f32[16,8,256]{2,1,0:T(8,128)S(1)} all-to-all(f32[16,8,256]{2,1,0:T(8,128)S(1)} %broadcast_in_dim.14), channel_id=1, replica_groups=mesh['zh'=2,'x'=4,'y'=8,'zl'=6,'c'=2] {'y','c'}, dimensions={0} | all-to-all | bytes 262144 | tf_op jit(solution)/shard_map/all_to_all | solution.py:17
  164.8 0.7 copy.11
  (4 shorter events, 0.1 us)
Async XLA Ops:
  0.6 74.9 %copy-start = (bf16[24,96,768]{2,1,0:T(8,128)(2,1)S(1)}, bf16[24,96,768]{2,1,0:T(8,128)(2,1)}, u32[]{:S(2)}) copy-start(bf16[24,96,768]{2,1,0:T(8,128)(2,1)} %param.9) | copy-start | bytes 10616836
  57.3 9.3 %collective-permute-start = (bf16[1152,4,128]{2,1,0:T(4,128)(2,1)}, bf16[1152,4,128]{2,1,0:T(4,128)(2,1)}, u32[]{:S(2)}, u32[]{:S(2)}) collective-permute-start(bf16[1152,4,128]{2,1,0:T(4,128)(2,1)} %bitcast.3.first_ref), channel_id=1, source_target_pairs={{0,1},{1,0},{2,3},{3,2},{4,5},{5,4},{6,7},{7,6},{8,9},{9,8},{10,11... | collective-permute-start | bytes 3538952 | tf_op jit(solution)/shard_map/ppermute | solution.py:151
  66.6 0.7 copy-start.2
  70.6 4.7 %collective-permute-start.1 = (bf16[576,4,128]{2,1,0:T(4,128)(2,1)S(1)}, bf16[576,4,128]{2,1,0:T(4,128)(2,1)S(1)}, u32[]{:S(2)}, u32[]{:S(2)}) collective-permute-start(bf16[576,4,128]{2,1,0:T(4,128)(2,1)S(1)} %shard_map.88), channel_id=1, source_target_pairs={{576,672},{672,576},{577,673},{673,577},{578,674},{674,578},{579,6... | collective-permute-start | bytes 1769480 | tf_op jit(solution)/shard_map/ppermute | solution.py:153
  71.3 0.7 copy-start.1
  87.0 33.8 %copy-start.3 = (bf16[768,256]{1,0:T(8,128)(2,1)S(1)}, bf16[768,256]{1,0:T(8,128)(2,1)}, u32[]{:S(2)}) copy-start(bf16[768,256]{1,0:T(8,128)(2,1)} %param.12) | copy-start | bytes 1179652
  87.0 23.4 %collective-permute-start.2 = (bf16[32,768]{1,0:T(8,128)(2,1)}, bf16[32,768]{1,0:T(8,128)(2,1)S(1)}, u32[]{:S(2)}, u32[]{:S(2)}) collective-permute-start(bf16[32,768]{1,0:T(8,128)(2,1)} %reduce_sum.30), channel_id=1, source_target_pairs={{0,384},{384,0},{1,385},{385,1},{2,386},{386,2},{3,387},{387,3},{4... | collective-permute-start | bytes 147464 | tf_op jit(solution)/shard_map/ppermute | solution.py:164

commit v5 on v4

--- a/solution.py
+++ b/solution.py
@@ -20,6 +20,13 @@
 def spread(value, axes):
     copies = jnp.broadcast_to(value[None], (lax.axis_size(axes),) + value.shape)
     return exchange(copies, axes)
+
+
+def added(terms):
+    total = terms[0].astype(jnp.float32)
+    for number in range(1, terms.shape[0]):
+        total = total + terms[number].astype(jnp.float32)
+    return total
 
 
 def vmem():
@@ -160,7 +167,7 @@
         picked, adj_tiles, (((0, 1), (0, 1)), ((), ())), preferred_element_type=jnp.float32
     ).astype(jnp.bfloat16)
     terms = exchange(partial_value, "x").reshape(lax.axis_size("x"), -1, block_rows)
-    near = jnp.sum(terms.astype(jnp.float32), axis=0).astype(jnp.bfloat16)
+    near = added(terms).astype(jnp.bfloat16)
     far = lax.ppermute(near, "zh", [(0, 1), (1, 0)])
     own_feats = (near.astype(jnp.float32) + far.astype(jnp.float32)).astype(jnp.bfloat16)
     aggregated = spread(own_feats, "x").reshape(feat_width, block_rows)
@@ -175,8 +182,8 @@
     local_grad = jnp.dot(aggregated, masked, preferred_element_type=jnp.float32)
 
     ring_terms = exchange(local_grad, ("y", "c")).reshape(lax.axis_size(("y", "c")), -1, hid)
-    line_terms = spread(jnp.sum(ring_terms, axis=0), "zl")
-    own_grad = jnp.sum(line_terms.reshape((-1,) + ring_terms.shape[1:]), axis=0)
+    line_terms = spread(added(ring_terms), "zl")
+    own_grad = added(line_terms.reshape((-1,) + ring_terms.shape[1:]))
     weight_grad = spread(own_grad, ("y", "c")).reshape(feat_width, hid)
     return (activated, weight_grad)
 

time: 166 us -> 160 us (0.964)
  other arithmetic: 4.44 us -> 0.4 us
    reduce_sum x3 -> x0, other arithmetic: 3.32 us -> none  [the longest x1 1.59 us: on_device(): near = jnp.sum(terms.astype(jnp.float32), axis=0).astype(jnp.bfloat16)]
where the time goes in v5:
time: 160 us
  blocking collectives  113 us (71%)
  starting transfers between devices  28.7 us (18%)
  Pallas kernels  8.43 us (5%)
  local copies, waits for them, and re-layouts  3.22 us (2%)
  matrix products  2.29 us (1%)
  waiting for transfers between devices  1.78 us (1%)
    all_to_all x7, blocking collectives, exchange(): return lax.all_to_all(pieces, axes, split_axis=0, concat_axis=0, tiled=True)  113 us
    ppermute x1, starting transfers between devices, on_device(): far = lax.ppermute(near, 'zh', [(0, 1), (1, 0)])  21.5 us
    ppermute x1, starting transfers between devices, on_device(): other_core = lax.ppermute(same_core, 'c', [(0, 1), (1, 0)])  6.54 us
    pallas_call x2, Pallas kernels, pick_parts(): pl.pallas_call(pick_kernel, out_shape=jax.ShapeDtypeStruct((count,) + par...  6.45 us
  transfers between devices with their start and end apart: 3, of which 2 were waited for; matrix products, arithmetic and copies ran while one was open for 0% of the time, Pallas kernels for 3%

profile of v5, /device:TPU:1, one launch (start us, length us, event | category | flops | bytes accessed | tf_op | source)
XLA Modules:
  0.0 159.6 jit_solution(12433339343964446234)
XLA Ops:
  0.6 0.0 copy-start
  0.7 0.9 constant_dynamic-slice_fusion
  1.6 20.9 %all_to_all.40 = bf16[6,96,128]{2,1,0:T(8,128)(2,1)S(1)} all-to-all(bf16[6,96,128]{2,1,0:T(8,128)(2,1)S(1)} %broadcast_in_dim.14), channel_id=1, replica_groups=mesh['zh'=2,'x'=4,'y'=8,'zl'=6,'c'=2] {'zl'}, dimensions={0} | all-to-all | bytes 294912 | tf_op jit(solution)/shard_map/all_to_all | solution.py:17
  22.5 0.2 broadcast_in_dim.15
  22.7 34.6 %all_to_all.41 = bf16[8,6,96,128]{3,2,1,0:T(8,128)(2,1)} all-to-all(bf16[8,6,96,128]{3,2,1,0:T(8,128)(2,1)S(1)} %broadcast_in_dim.15), channel_id=1, replica_groups=mesh['zh'=2,'x'=4,'y'=8,'zl'=6,'c'=2] {'y'}, dimensions={0} | all-to-all | bytes 2359296 | tf_op jit(solution)/shard_map/all_to_all | solution.py:17
  57.3 6.5 %collective-permute-start = (bf16[1152,4,128]{2,1,0:T(4,128)(2,1)}, bf16[1152,4,128]{2,1,0:T(4,128)(2,1)}, u32[]{:S(2)}, u32[]{:S(2)}) collective-permute-start(bf16[1152,4,128]{2,1,0:T(4,128)(2,1)} %bitcast.3.first_ref), channel_id=1, source_target_pairs={{0,1},{1,0},{2,3},{3,2},{4,5},{5,4},{6,7},{7,6},{8,9},{9,8},{10,11... | collective-permute-start | bytes 3538952 | tf_op jit(solution)/shard_map/ppermute | solution.py:158
  64.5 2.0 %shard_map.86 = (s32[24,24]{1,0:T(8,128)}, s32[24,24]{1,0:T(8,128)}) custom-call(s32[1]{0:T(128)} %bitcast.group_ref, s32[1]{0:T(128)} %bitcast.1.core_ref, s32[1]{0:T(128)S(6)} %copy.10.live_ref, s32[1,24]{1,0:T(1,128)} %column_ref.1, s32[48,96]{1,0:T(8,128)} %bitcast.34, s32[1,24]{1,0:T(1,128)} %column_ref.1), custom_call_target="tpu_custom_call" | custom-call | flops 4000000 | bytes 50000 | tf_op jit(solution)/shard_map/pallas_call | solution.py:97
  66.5 0.2 collective-permute-done.second_ref
  66.6 0.0 copy-start.2
  66.6 0.7 copy-done.2
  67.3 3.2 %shard_map.88 = bf16[576,4,128]{2,1,0:T(4,128)(2,1)S(1)} custom-call(s32[24,24]{1,0:T(8,128)S(1)} %copy-done.2, bf16[1152,4,128]{2,1,0:T(4,128)(2,1)} %bitcast.3.first_ref, bf16[1152,4,128]{2,1,0:T(4,128)(2,1)} %collective-permute-done.second_ref), custom_call_target="tpu_custom_call" | custom-call | flops 1000000 | bytes 3000000 | tf_op jit(solution)/shard_map/pallas_call | solution.py:129
  70.6 0.7 collective-permute-start.1
  71.3 0.0 copy-start.1
  71.3 0.7 copy-done.1
  72.0 3.2 %shard_map.87 = bf16[576,4,128]{2,1,0:T(4,128)(2,1)S(1)} custom-call(s32[24,24]{1,0:T(8,128)S(1)} %copy-done.1, bf16[1152,4,128]{2,1,0:T(4,128)(2,1)} %bitcast.3.first_ref, bf16[1152,4,128]{2,1,0:T(4,128)(2,1)} %collective-permute-done.second_ref), custom_call_target="tpu_custom_call" | custom-call | flops 1000000 | bytes 3000000 | tf_op jit(solution)/shard_map/pallas_call | solution.py:129
  75.2 0.0 copy-start.4
  75.2 0.0 collective-permute-done.1
  75.2 0.3 add.114
  75.6 0.0 copy-done
  75.6 0.7 fusion
  76.3 0.0 copy-start.3
  76.3 9.2 %all_to_all.42 = bf16[4,32,768]{2,1,0:T(8,128)(2,1)S(1)} all-to-all(bf16[4,32,768]{2,1,0:T(8,128)(2,1)S(1)} %bitcast.30), channel_id=1, replica_groups=mesh['zh'=2,'x'=4,'y'=8,'zl'=6,'c'=2] {'x'}, dimensions={0} | all-to-all | bytes 393216 | tf_op jit(solution)/shard_map/all_to_all | solution.py:17
  85.5 21.5 %collective-permute-start.2 = (bf16[32,768]{1,0:T(8,128)(2,1)S(1)}, bf16[32,768]{1,0:T(8,128)(2,1)S(1)}, u32[]{:S(2)}, u32[]{:S(2)}) collective-permute-start(bf16[32,768]{1,0:T(8,128)(2,1)S(1)} %fusion.3), channel_id=1, source_target_pairs={{0,384},{384,0},{1,385},{385,1},{2,386},{386,2},{3,387},{387,3},{4... | collective-permute-start | bytes 147464 | tf_op jit(solution)/shard_map/ppermute | solution.py:171
  107.0 1.6 %collective-permute-done.2 = bf16[32,768]{1,0:T(8,128)(2,1)S(1)} collective-permute-done((bf16[32,768]{1,0:T(8,128)(2,1)S(1)}, bf16[32,768]{1,0:T(8,128)(2,1)S(1)}, u32[]{:S(2)}, u32[]{:S(2)}) %collective-permute-start.2) | collective-permute-done | bytes 49184 | tf_op jit(solution)/shard_map/ppermute | solution.py:171
  108.7 7.5 %all_to_all.43 = bf16[4,32,768]{2,1,0:T(8,128)(2,1)S(1)} all-to-all(bf16[4,32,768]{2,1,0:T(8,128)(2,1)S(1)} %broadcast_in_dim.16), channel_id=1, replica_groups=mesh['zh'=2,'x'=4,'y'=8,'zl'=6,'c'=2] {'x'}, dimensions={0} | all-to-all | bytes 393216 | tf_op jit(solution)/shard_map/all_to_all | solution.py:17
  116.2 0.0 copy-done.4
  116.2 1.1 multiply_convert_fusion.1
  117.4 0.0 copy-done.3
  117.4 0.5 fusion.1
  117.8 16.1 %all_to_all.44 = f32[16,8,256]{2,1,0:T(8,128)S(1)} all-to-all(f32[16,8,256]{2,1,0:T(8,128)S(1)} %fusion.1), channel_id=1, replica_groups=mesh['zh'=2,'x'=4,'y'=8,'zl'=6,'c'=2] {'y','c'}, dimensions={0} | all-to-all | bytes 262144 | tf_op jit(solution)/shard_map/all_to_all | solution.py:17
  134.0 11.9 %all_to_all.45 = f32[6,8,256]{2,1,0:T(8,128)S(1)} all-to-all(f32[6,8,256]{2,1,0:T(8,128)S(1)} %broadcast_in_dim.18), channel_id=1, replica_groups=mesh['zh'=2,'x'=4,'y'=8,'zl'=6,'c'=2] {'zl'}, dimensions={0} | all-to-all | bytes 98304 | tf_op jit(solution)/shard_map/all_to_all | solution.py:17
  145.9 13.0 %all_to_all.46 = f32[16,8,256]{2,1,0:T(8,128)S(1)} all-to-all(f32[16,8,256]{2,1,0:T(8,128)S(1)} %broadcast_in_dim.40), channel_id=1, replica_groups=mesh['zh'=2,'x'=4,'y'=8,'zl'=6,'c'=2] {'y','c'}, dimensions={0} | all-to-all | bytes 262144 | tf_op jit(solution)/shard_map/all_to_all | solution.py:17
  158.9 0.7 copy.11
  (8 shorter events, 0.1 us)
Async XLA Ops:
  0.6 74.9 %copy-start = (bf16[24,96,768]{2,1,0:T(8,128)(2,1)S(1)}, bf16[24,96,768]{2,1,0:T(8,128)(2,1)}, u32[]{:S(2)}) copy-start(bf16[24,96,768]{2,1,0:T(8,128)(2,1)} %param.9) | copy-start | bytes 10616836
  57.3 9.3 %collective-permute-start = (bf16[1152,4,128]{2,1,0:T(4,128)(2,1)}, bf16[1152,4,128]{2,1,0:T(4,128)(2,1)}, u32[]{:S(2)}, u32[]{:S(2)}) collective-permute-start(bf16[1152,4,128]{2,1,0:T(4,128)(2,1)} %bitcast.3.first_ref), channel_id=1, source_target_pairs={{0,1},{1,0},{2,3},{3,2},{4,5},{5,4},{6,7},{7,6},{8,9},{9,8},{10,11... | collective-permute-start | bytes 3538952 | tf_op jit(solution)/shard_map/ppermute | solution.py:158
  66.6 0.7 copy-start.2
  70.6 4.7 %collective-permute-start.1 = (bf16[576,4,128]{2,1,0:T(4,128)(2,1)S(1)}, bf16[576,4,128]{2,1,0:T(4,128)(2,1)S(1)}, u32[]{:S(2)}, u32[]{:S(2)}) collective-permute-start(bf16[576,4,128]{2,1,0:T(4,128)(2,1)S(1)} %shard_map.88), channel_id=1, source_target_pairs={{576,672},{672,576},{577,673},{673,577},{578,674},{674,578},{579,6... | collective-permute-start | bytes 1769480 | tf_op jit(solution)/shard_map/ppermute | solution.py:160
  71.3 0.7 copy-start.1
  75.2 41.0 %copy-start.4 = (bf16[128,256]{1,0:T(8,128)(2,1)S(1)}, bf16[128,256]{1,0:T(8,128)(2,1)}, u32[]{:S(2)}) copy-start(bf16[128,256]{1,0:T(8,128)(2,1)} %param.13) | copy-start | bytes 196612
  76.3 41.1 %copy-start.3 = (bf16[768,256]{1,0:T(8,128)(2,1)S(1)}, bf16[768,256]{1,0:T(8,128)(2,1)}, u32[]{:S(2)}) copy-start(bf16[768,256]{1,0:T(8,128)(2,1)} %param.12) | copy-start | bytes 1179652
  85.5 23.1 %collective-permute-start.2 = (bf16[32,768]{1,0:T(8,128)(2,1)S(1)}, bf16[32,768]{1,0:T(8,128)(2,1)S(1)}, u32[]{:S(2)}, u32[]{:S(2)}) collective-permute-start(bf16[32,768]{1,0:T(8,128)(2,1)S(1)} %fusion.3), channel_id=1, source_target_pairs={{0,384},{384,0},{1,385},{385,1},{2,386},{386,2},{3,387},{387,3},{4... | collective-permute-start | bytes 147464 | tf_op jit(solution)/shard_map/ppermute | solution.py:171

commit v6 on v5

--- a/solution.py
+++ b/solution.py
@@ -181,7 +181,7 @@
     masked = (grad_out.astype(jnp.float32) * slope).astype(jnp.bfloat16)
     local_grad = jnp.dot(aggregated, masked, preferred_element_type=jnp.float32)
 
-    ring_terms = exchange(local_grad, ("y", "c")).reshape(lax.axis_size(("y", "c")), -1, hid)
+    ring_terms = exchange(local_grad.astype(jnp.bfloat16), ("y", "c")).reshape(lax.axis_size(("y", "c")), -1, hid)
     line_terms = spread(added(ring_terms), "zl")
     own_grad = added(line_terms.reshape((-1,) + ring_terms.shape[1:]))
     weight_grad = spread(own_grad, ("y", "c")).reshape(feat_width, hid)

time: 160 us -> 159 us (level)
  no operation moved by 1% of the time
where the time goes in v6:
time: 159 us; the launch traced here: 158 us
  blocking collectives  112 us (70%)
  starting transfers between devices  28.7 us (18%)
  Pallas kernels  8.43 us (5%)
  local copies, waits for them, and re-layouts  3.22 us (2%)
  matrix products  2.28 us (1%)
  waiting for transfers between devices  1.78 us (1%)
    all_to_all x7, blocking collectives, exchange(): return lax.all_to_all(pieces, axes, split_axis=0, concat_axis=0, tiled=True)  112 us
    ppermute x1, starting transfers between devices, on_device(): far = lax.ppermute(near, 'zh', [(0, 1), (1, 0)])  21.5 us
    ppermute x1, starting transfers between devices, on_device(): other_core = lax.ppermute(same_core, 'c', [(0, 1), (1, 0)])  6.54 us
    pallas_call x2, Pallas kernels, pick_parts(): pl.pallas_call(pick_kernel, out_shape=jax.ShapeDtypeStruct((count,) + par...  6.45 us
  transfers between devices with their start and end apart: 3, of which 2 were waited for; matrix products, arithmetic and copies ran while one was open for 0% of the time, Pallas kernels for 3%

profile of v6, /device:TPU:1, one launch (start us, length us, event | category | flops | bytes accessed | tf_op | source)
XLA Modules:
  0.0 158.4 jit_solution(18129843174829926894)
XLA Ops:
  0.6 0.0 copy-start
  0.7 0.9 constant_dynamic-slice_fusion
  1.6 20.9 %all_to_all.43 = bf16[6,96,128]{2,1,0:T(8,128)(2,1)S(1)} all-to-all(bf16[6,96,128]{2,1,0:T(8,128)(2,1)S(1)} %broadcast_in_dim.14), channel_id=1, replica_groups=mesh['zh'=2,'x'=4,'y'=8,'zl'=6,'c'=2] {'zl'}, dimensions={0} | all-to-all | bytes 294912 | tf_op jit(solution)/shard_map/all_to_all | solution.py:17
  22.5 0.2 broadcast_in_dim.15
  22.7 34.6 %all_to_all.44 = bf16[8,6,96,128]{3,2,1,0:T(8,128)(2,1)} all-to-all(bf16[8,6,96,128]{3,2,1,0:T(8,128)(2,1)S(1)} %broadcast_in_dim.15), channel_id=1, replica_groups=mesh['zh'=2,'x'=4,'y'=8,'zl'=6,'c'=2] {'y'}, dimensions={0} | all-to-all | bytes 2359296 | tf_op jit(solution)/shard_map/all_to_all | solution.py:17
  57.3 6.5 %collective-permute-start = (bf16[1152,4,128]{2,1,0:T(4,128)(2,1)}, bf16[1152,4,128]{2,1,0:T(4,128)(2,1)}, u32[]{:S(2)}, u32[]{:S(2)}) collective-permute-start(bf16[1152,4,128]{2,1,0:T(4,128)(2,1)} %bitcast.3.first_ref), channel_id=1, source_target_pairs={{0,1},{1,0},{2,3},{3,2},{4,5},{5,4},{6,7},{7,6},{8,9},{9,8},{10,11... | collective-permute-start | bytes 3538952 | tf_op jit(solution)/shard_map/ppermute | solution.py:158
  64.5 2.0 %shard_map.86 = (s32[24,24]{1,0:T(8,128)}, s32[24,24]{1,0:T(8,128)}) custom-call(s32[1]{0:T(128)} %bitcast.group_ref, s32[1]{0:T(128)} %bitcast.1.core_ref, s32[1]{0:T(128)S(6)} %copy.10.live_ref, s32[1,24]{1,0:T(1,128)} %column_ref.1, s32[48,96]{1,0:T(8,128)} %bitcast.32, s32[1,24]{1,0:T(1,128)} %column_ref.1), custom_call_target="tpu_custom_call" | custom-call | flops 4000000 | bytes 50000 | tf_op jit(solution)/shard_map/pallas_call | solution.py:97
  66.5 0.2 collective-permute-done.second_ref
  66.6 0.0 copy-start.2
  66.6 0.7 copy-done.2
  67.3 3.2 %shard_map.88 = bf16[576,4,128]{2,1,0:T(4,128)(2,1)S(1)} custom-call(s32[24,24]{1,0:T(8,128)S(1)} %copy-done.2, bf16[1152,4,128]{2,1,0:T(4,128)(2,1)} %bitcast.3.first_ref, bf16[1152,4,128]{2,1,0:T(4,128)(2,1)} %collective-permute-done.second_ref), custom_call_target="tpu_custom_call" | custom-call | flops 1000000 | bytes 3000000 | tf_op jit(solution)/shard_map/pallas_call | solution.py:129
  70.6 0.7 collective-permute-start.1
  71.3 0.0 copy-start.1
  71.3 0.7 copy-done.1
  72.0 3.2 %shard_map.87 = bf16[576,4,128]{2,1,0:T(4,128)(2,1)S(1)} custom-call(s32[24,24]{1,0:T(8,128)S(1)} %copy-done.1, bf16[1152,4,128]{2,1,0:T(4,128)(2,1)} %bitcast.3.first_ref, bf16[1152,4,128]{2,1,0:T(4,128)(2,1)} %collective-permute-done.second_ref), custom_call_target="tpu_custom_call" | custom-call | flops 1000000 | bytes 3000000 | tf_op jit(solution)/shard_map/pallas_call | solution.py:129
  75.2 0.0 copy-start.4
  75.2 0.0 collective-permute-done.1
  75.2 0.3 add.114
  75.6 0.0 copy-done
  75.6 0.7 fusion
  76.3 0.0 copy-start.3
  76.3 9.2 %all_to_all.45 = bf16[4,32,768]{2,1,0:T(8,128)(2,1)S(1)} all-to-all(bf16[4,32,768]{2,1,0:T(8,128)(2,1)S(1)} %bitcast.28), channel_id=1, replica_groups=mesh['zh'=2,'x'=4,'y'=8,'zl'=6,'c'=2] {'x'}, dimensions={0} | all-to-all | bytes 393216 | tf_op jit(solution)/shard_map/all_to_all | solution.py:17
  85.5 21.5 %collective-permute-start.2 = (bf16[32,768]{1,0:T(8,128)(2,1)S(1)}, bf16[32,768]{1,0:T(8,128)(2,1)S(1)}, u32[]{:S(2)}, u32[]{:S(2)}) collective-permute-start(bf16[32,768]{1,0:T(8,128)(2,1)S(1)} %fusion.2), channel_id=1, source_target_pairs={{0,384},{384,0},{1,385},{385,1},{2,386},{386,2},{3,387},{387,3},{4... | collective-permute-start | bytes 147464 | tf_op jit(solution)/shard_map/ppermute | solution.py:171
  107.0 1.6 %collective-permute-done.2 = bf16[32,768]{1,0:T(8,128)(2,1)S(1)} collective-permute-done((bf16[32,768]{1,0:T(8,128)(2,1)S(1)}, bf16[32,768]{1,0:T(8,128)(2,1)S(1)}, u32[]{:S(2)}, u32[]{:S(2)}) %collective-permute-start.2) | collective-permute-done | bytes 49184 | tf_op jit(solution)/shard_map/ppermute | solution.py:171
  108.7 7.5 %all_to_all.46 = bf16[4,32,768]{2,1,0:T(8,128)(2,1)S(1)} all-to-all(bf16[4,32,768]{2,1,0:T(8,128)(2,1)S(1)} %broadcast_in_dim.16), channel_id=1, replica_groups=mesh['zh'=2,'x'=4,'y'=8,'zl'=6,'c'=2] {'x'}, dimensions={0} | all-to-all | bytes 393216 | tf_op jit(solution)/shard_map/all_to_all | solution.py:17
  116.2 0.0 copy-done.4
  116.2 1.1 multiply_convert_fusion.1
  117.4 0.0 copy-done.3
  117.4 0.4 fusion.1
  117.8 14.7 %all_to_all.47 = bf16[16,8,256]{2,1,0:T(8,128)(2,1)S(1)} all-to-all(bf16[16,8,256]{2,1,0:T(8,128)(2,1)S(1)} %fusion.1), channel_id=1, replica_groups=mesh['zh'=2,'x'=4,'y'=8,'zl'=6,'c'=2] {'y','c'}, dimensions={0} | all-to-all | bytes 131072 | tf_op jit(solution)/shard_map/all_to_all | solution.py:17
  132.6 11.9 %all_to_all.48 = f32[6,8,256]{2,1,0:T(8,128)S(1)} all-to-all(f32[6,8,256]{2,1,0:T(8,128)S(1)} %broadcast_in_dim.18), channel_id=1, replica_groups=mesh['zh'=2,'x'=4,'y'=8,'zl'=6,'c'=2] {'zl'}, dimensions={0} | all-to-all | bytes 98304 | tf_op jit(solution)/shard_map/all_to_all | solution.py:17
  144.5 13.2 %all_to_all.49 = f32[16,8,256]{2,1,0:T(8,128)S(1)} all-to-all(f32[16,8,256]{2,1,0:T(8,128)S(1)} %broadcast_in_dim.40), channel_id=1, replica_groups=mesh['zh'=2,'x'=4,'y'=8,'zl'=6,'c'=2] {'y','c'}, dimensions={0} | all-to-all | bytes 262144 | tf_op jit(solution)/shard_map/all_to_all | solution.py:17
  157.7 0.7 copy.11
  (8 shorter events, 0.1 us)
Async XLA Ops:
  0.6 74.9 %copy-start = (bf16[24,96,768]{2,1,0:T(8,128)(2,1)S(1)}, bf16[24,96,768]{2,1,0:T(8,128)(2,1)}, u32[]{:S(2)}) copy-start(bf16[24,96,768]{2,1,0:T(8,128)(2,1)} %param.9) | copy-start | bytes 10616836
  57.3 9.3 %collective-permute-start = (bf16[1152,4,128]{2,1,0:T(4,128)(2,1)}, bf16[1152,4,128]{2,1,0:T(4,128)(2,1)}, u32[]{:S(2)}, u32[]{:S(2)}) collective-permute-start(bf16[1152,4,128]{2,1,0:T(4,128)(2,1)} %bitcast.3.first_ref), channel_id=1, source_target_pairs={{0,1},{1,0},{2,3},{3,2},{4,5},{5,4},{6,7},{7,6},{8,9},{9,8},{10,11... | collective-permute-start | bytes 3538952 | tf_op jit(solution)/shard_map/ppermute | solution.py:158
  66.6 0.7 copy-start.2
  70.6 4.7 %collective-permute-start.1 = (bf16[576,4,128]{2,1,0:T(4,128)(2,1)S(1)}, bf16[576,4,128]{2,1,0:T(4,128)(2,1)S(1)}, u32[]{:S(2)}, u32[]{:S(2)}) collective-permute-start(bf16[576,4,128]{2,1,0:T(4,128)(2,1)S(1)} %shard_map.88), channel_id=1, source_target_pairs={{576,672},{672,576},{577,673},{673,577},{578,674},{674,578},{579,6... | collective-permute-start | bytes 1769480 | tf_op jit(solution)/shard_map/ppermute | solution.py:160
  71.3 0.7 copy-start.1
  75.2 41.0 %copy-start.4 = (bf16[128,256]{1,0:T(8,128)(2,1)S(1)}, bf16[128,256]{1,0:T(8,128)(2,1)}, u32[]{:S(2)}) copy-start(bf16[128,256]{1,0:T(8,128)(2,1)} %param.13) | copy-start | bytes 196612
  76.3 41.1 %copy-start.3 = (bf16[768,256]{1,0:T(8,128)(2,1)S(1)}, bf16[768,256]{1,0:T(8,128)(2,1)}, u32[]{:S(2)}) copy-start(bf16[768,256]{1,0:T(8,128)(2,1)} %param.12) | copy-start | bytes 1179652
  85.5 23.1 %collective-permute-start.2 = (bf16[32,768]{1,0:T(8,128)(2,1)S(1)}, bf16[32,768]{1,0:T(8,128)(2,1)S(1)}, u32[]{:S(2)}, u32[]{:S(2)}) collective-permute-start(bf16[32,768]{1,0:T(8,128)(2,1)S(1)} %fusion.2), channel_id=1, source_target_pairs={{0,384},{384,0},{1,385},{385,1},{2,386},{386,2},{3,387},{387,3},{4... | collective-permute-start | bytes 147464 | tf_op jit(solution)/shard_map/ppermute | solution.py:171

commit v7 on v6

--- a/solution.py
+++ b/solution.py
@@ -104,13 +104,16 @@
     )(*role, columns, dest_plan.T, columns)
 
 
-def pick_kernel(place_ref, first_ref, second_ref, out_ref, held_ref, sems):
+def pick_kernel(list_ref, first_ref, second_ref, out_ref, held_ref, place_ref, sems):
     half = first_ref.shape[0]
     first = pltpu.make_async_copy(first_ref, held_ref.at[pl.ds(0, half)], sems.at[0])
     second = pltpu.make_async_copy(second_ref, held_ref.at[pl.ds(half, half)], sems.at[1])
+    listed = pltpu.make_async_copy(list_ref, place_ref, sems.at[2])
+    listed.start()
     first.start()
     second.start()
     held_ref[2 * half] = jnp.zeros(held_ref.shape[1:], held_ref.dtype)
+    listed.wait()
     first.wait()
     second.wait()
     orders, slots = place_ref.shape
@@ -129,11 +132,12 @@
     return pl.pallas_call(
         pick_kernel,
         out_shape=jax.ShapeDtypeStruct((count,) + part, first.dtype),
-        in_specs=[smem()] + [pl.BlockSpec(memory_space=pl.ANY)] * 2,
+        in_specs=[pl.BlockSpec(memory_space=pl.ANY)] * 3,
         out_specs=vmem(),
         scratch_shapes=[
             pltpu.VMEM((2 * first.shape[0] + 8,) + part, first.dtype),
-            pltpu.SemaphoreType.DMA((2,)),
+            pltpu.SMEM(places.shape, jnp.int32),
+            pltpu.SemaphoreType.DMA((3,)),
         ],
         compiler_params=pltpu.CompilerParams(vmem_limit_bytes=8 * 1024 * 1024),
         cost_estimate=pl.CostEstimate(flops=1000000, bytes_accessed=3000000, transcendentals=0),

time: 159 us -> 158 us (level)
  no operation moved by 1% of the time
where the time goes in v7:
time: 158 us
  blocking collectives  112 us (71%)
  starting transfers between devices  29.4 us (19%)
  Pallas kernels  6.98 us (4%)
  local copies, waits for them, and re-layouts  3.22 us (2%)
  matrix products  2.28 us (1%)
  waiting for transfers between devices  1.78 us (1%)
    all_to_all x7, blocking collectives, exchange(): return lax.all_to_all(pieces, axes, split_axis=0, concat_axis=0, tiled=True)  112 us
    ppermute x1, starting transfers between devices, on_device(): far = lax.ppermute(near, 'zh', [(0, 1), (1, 0)])  22.2 us
    ppermute x1, starting transfers between devices, on_device(): other_core = lax.ppermute(same_core, 'c', [(0, 1), (1, 0)])  6.54 us
    pallas_call x2, Pallas kernels, pick_parts(): pl.pallas_call(pick_kernel, out_shape=jax.ShapeDtypeStruct((count,) + par...  5 us
  transfers between devices with their start and end apart: 3, of which 2 were waited for; matrix products, arithmetic and copies ran while one was open for 0% of the time, Pallas kernels for 3%

profile of v7, /device:TPU:1, one launch (start us, length us, event | category | flops | bytes accessed | tf_op | source)
XLA Modules:
  0.0 157.6 jit_solution(12310850732560799604)
XLA Ops:
  0.6 0.0 copy-start
  0.7 0.9 constant_dynamic-slice_fusion
  1.6 20.9 %all_to_all.43 = bf16[6,96,128]{2,1,0:T(8,128)(2,1)S(1)} all-to-all(bf16[6,96,128]{2,1,0:T(8,128)(2,1)S(1)} %broadcast_in_dim.14), channel_id=1, replica_groups=mesh['zh'=2,'x'=4,'y'=8,'zl'=6,'c'=2] {'zl'}, dimensions={0} | all-to-all | bytes 294912 | tf_op jit(solution)/shard_map/all_to_all | solution.py:17
  22.5 0.2 broadcast_in_dim.15
  22.7 34.6 %all_to_all.44 = bf16[8,6,96,128]{3,2,1,0:T(8,128)(2,1)} all-to-all(bf16[8,6,96,128]{3,2,1,0:T(8,128)(2,1)S(1)} %broadcast_in_dim.15), channel_id=1, replica_groups=mesh['zh'=2,'x'=4,'y'=8,'zl'=6,'c'=2] {'y'}, dimensions={0} | all-to-all | bytes 2359296 | tf_op jit(solution)/shard_map/all_to_all | solution.py:17
  57.3 6.5 %collective-permute-start = (bf16[1152,4,128]{2,1,0:T(4,128)(2,1)}, bf16[1152,4,128]{2,1,0:T(4,128)(2,1)}, u32[]{:S(2)}, u32[]{:S(2)}) collective-permute-start(bf16[1152,4,128]{2,1,0:T(4,128)(2,1)} %bitcast.3.first_ref), channel_id=1, source_target_pairs={{0,1},{1,0},{2,3},{3,2},{4,5},{5,4},{6,7},{7,6},{8,9},{9,8},{10,11... | collective-permute-start | bytes 3538952 | tf_op jit(solution)/shard_map/ppermute | solution.py:162
  64.5 2.0 %shard_map.86 = (s32[24,24]{1,0:T(8,128)}, s32[24,24]{1,0:T(8,128)}) custom-call(s32[1]{0:T(128)} %bitcast.group_ref, s32[1]{0:T(128)} %bitcast.1.core_ref, s32[1]{0:T(128)S(6)} %copy.10.live_ref, s32[1,24]{1,0:T(1,128)} %column_ref.1, s32[48,96]{1,0:T(8,128)} %bitcast.32, s32[1,24]{1,0:T(1,128)} %column_ref.1), custom_call_target="tpu_custom_call" | custom-call | flops 4000000 | bytes 50000 | tf_op jit(solution)/shard_map/pallas_call | solution.py:97
  66.5 0.2 collective-permute-done.second_ref
  66.6 0.0 copy-start.2
  66.6 0.7 copy-done.2
  67.3 2.5 %shard_map.88 = bf16[576,4,128]{2,1,0:T(4,128)(2,1)S(1)} custom-call(s32[24,24]{1,0:T(8,128)S(1)} %copy-done.2, bf16[1152,4,128]{2,1,0:T(4,128)(2,1)} %bitcast.3.first_ref, bf16[1152,4,128]{2,1,0:T(4,128)(2,1)} %collective-permute-done.second_ref), custom_call_target="tpu_custom_call" | custom-call | flops 1000000 | bytes 3000000 | tf_op jit(solution)/shard_map/pallas_call | solution.py:132
  69.8 0.7 collective-permute-start.1
  70.6 0.0 copy-start.1
  70.6 0.7 copy-done.1
  71.3 2.5 %shard_map.87 = bf16[576,4,128]{2,1,0:T(4,128)(2,1)S(1)} custom-call(s32[24,24]{1,0:T(8,128)S(1)} %copy-done.1, bf16[1152,4,128]{2,1,0:T(4,128)(2,1)} %bitcast.3.first_ref, bf16[1152,4,128]{2,1,0:T(4,128)(2,1)} %collective-permute-done.second_ref), custom_call_target="tpu_custom_call" | custom-call | flops 1000000 | bytes 3000000 | tf_op jit(solution)/shard_map/pallas_call | solution.py:132
  73.8 0.0 copy-start.4
  73.8 0.0 collective-permute-done.1
  73.8 0.3 add.114
  74.1 0.0 copy-done
  74.1 0.7 fusion
  74.8 0.0 copy-start.3
  74.8 9.2 %all_to_all.45 = bf16[4,32,768]{2,1,0:T(8,128)(2,1)S(1)} all-to-all(bf16[4,32,768]{2,1,0:T(8,128)(2,1)S(1)} %bitcast.28), channel_id=1, replica_groups=mesh['zh'=2,'x'=4,'y'=8,'zl'=6,'c'=2] {'x'}, dimensions={0} | all-to-all | bytes 393216 | tf_op jit(solution)/shard_map/all_to_all | solution.py:17
  84.1 22.2 %collective-permute-start.2 = (bf16[32,768]{1,0:T(8,128)(2,1)S(1)}, bf16[32,768]{1,0:T(8,128)(2,1)S(1)}, u32[]{:S(2)}, u32[]{:S(2)}) collective-permute-start(bf16[32,768]{1,0:T(8,128)(2,1)S(1)} %fusion.2), channel_id=1, source_target_pairs={{0,384},{384,0},{1,385},{385,1},{2,386},{386,2},{3,387},{387,3},{4... | collective-permute-start | bytes 147464 | tf_op jit(solution)/shard_map/ppermute | solution.py:175
  106.3 1.6 %collective-permute-done.2 = bf16[32,768]{1,0:T(8,128)(2,1)S(1)} collective-permute-done((bf16[32,768]{1,0:T(8,128)(2,1)S(1)}, bf16[32,768]{1,0:T(8,128)(2,1)S(1)}, u32[]{:S(2)}, u32[]{:S(2)}) %collective-permute-start.2) | collective-permute-done | bytes 49184 | tf_op jit(solution)/shard_map/ppermute | solution.py:175
  108.0 7.5 %all_to_all.46 = bf16[4,32,768]{2,1,0:T(8,128)(2,1)S(1)} all-to-all(bf16[4,32,768]{2,1,0:T(8,128)(2,1)S(1)} %broadcast_in_dim.16), channel_id=1, replica_groups=mesh['zh'=2,'x'=4,'y'=8,'zl'=6,'c'=2] {'x'}, dimensions={0} | all-to-all | bytes 393216 | tf_op jit(solution)/shard_map/all_to_all | solution.py:17
  115.5 0.0 copy-done.4
  115.5 1.1 multiply_convert_fusion.1
  116.7 0.0 copy-done.3
  116.7 0.4 fusion.1
  117.1 14.7 %all_to_all.47 = bf16[16,8,256]{2,1,0:T(8,128)(2,1)S(1)} all-to-all(bf16[16,8,256]{2,1,0:T(8,128)(2,1)S(1)} %fusion.1), channel_id=1, replica_groups=mesh['zh'=2,'x'=4,'y'=8,'zl'=6,'c'=2] {'y','c'}, dimensions={0} | all-to-all | bytes 131072 | tf_op jit(solution)/shard_map/all_to_all | solution.py:17
  131.9 11.9 %all_to_all.48 = f32[6,8,256]{2,1,0:T(8,128)S(1)} all-to-all(f32[6,8,256]{2,1,0:T(8,128)S(1)} %broadcast_in_dim.18), channel_id=1, replica_groups=mesh['zh'=2,'x'=4,'y'=8,'zl'=6,'c'=2] {'zl'}, dimensions={0} | all-to-all | bytes 98304 | tf_op jit(solution)/shard_map/all_to_all | solution.py:17
  143.8 13.2 %all_to_all.49 = f32[16,8,256]{2,1,0:T(8,128)S(1)} all-to-all(f32[16,8,256]{2,1,0:T(8,128)S(1)} %broadcast_in_dim.40), channel_id=1, replica_groups=mesh['zh'=2,'x'=4,'y'=8,'zl'=6,'c'=2] {'y','c'}, dimensions={0} | all-to-all | bytes 262144 | tf_op jit(solution)/shard_map/all_to_all | solution.py:17
  157.0 0.7 copy.11
  (8 shorter events, 0.1 us)
Async XLA Ops:
  0.6 73.5 %copy-start = (bf16[24,96,768]{2,1,0:T(8,128)(2,1)S(1)}, bf16[24,96,768]{2,1,0:T(8,128)(2,1)}, u32[]{:S(2)}) copy-start(bf16[24,96,768]{2,1,0:T(8,128)(2,1)} %param.9) | copy-start | bytes 10616836
  57.3 9.3 %collective-permute-start = (bf16[1152,4,128]{2,1,0:T(4,128)(2,1)}, bf16[1152,4,128]{2,1,0:T(4,128)(2,1)}, u32[]{:S(2)}, u32[]{:S(2)}) collective-permute-start(bf16[1152,4,128]{2,1,0:T(4,128)(2,1)} %bitcast.3.first_ref), channel_id=1, source_target_pairs={{0,1},{1,0},{2,3},{3,2},{4,5},{5,4},{6,7},{7,6},{8,9},{9,8},{10,11... | collective-permute-start | bytes 3538952 | tf_op jit(solution)/shard_map/ppermute | solution.py:162
  66.6 0.7 copy-start.2
  69.8 3.9 %collective-permute-start.1 = (bf16[576,4,128]{2,1,0:T(4,128)(2,1)S(1)}, bf16[576,4,128]{2,1,0:T(4,128)(2,1)S(1)}, u32[]{:S(2)}, u32[]{:S(2)}) collective-permute-start(bf16[576,4,128]{2,1,0:T(4,128)(2,1)S(1)} %shard_map.88), channel_id=1, source_target_pairs={{576,672},{672,576},{577,673},{673,577},{578,674},{674,578},{579,6... | collective-permute-start | bytes 1769480 | tf_op jit(solution)/shard_map/ppermute | solution.py:164
  70.6 0.7 copy-start.1
  73.8 41.7 %copy-start.4 = (bf16[128,256]{1,0:T(8,128)(2,1)S(1)}, bf16[128,256]{1,0:T(8,128)(2,1)}, u32[]{:S(2)}) copy-start(bf16[128,256]{1,0:T(8,128)(2,1)} %param.13) | copy-start | bytes 196612
  74.8 41.8 %copy-start.3 = (bf16[768,256]{1,0:T(8,128)(2,1)S(1)}, bf16[768,256]{1,0:T(8,128)(2,1)}, u32[]{:S(2)}) copy-start(bf16[768,256]{1,0:T(8,128)(2,1)} %param.12) | copy-start | bytes 1179652
  84.1 23.8 %collective-permute-start.2 = (bf16[32,768]{1,0:T(8,128)(2,1)S(1)}, bf16[32,768]{1,0:T(8,128)(2,1)S(1)}, u32[]{:S(2)}, u32[]{:S(2)}) collective-permute-start(bf16[32,768]{1,0:T(8,128)(2,1)S(1)} %fusion.2), channel_id=1, source_target_pairs={{0,384},{384,0},{1,385},{385,1},{2,386},{386,2},{3,387},{387,3},{4... | collective-permute-start | bytes 147464 | tf_op jit(solution)/shard_map/ppermute | solution.py:175

commit v8 on v7

--- a/solution.py
+++ b/solution.py
@@ -186,7 +186,7 @@
     local_grad = jnp.dot(aggregated, masked, preferred_element_type=jnp.float32)
 
     ring_terms = exchange(local_grad.astype(jnp.bfloat16), ("y", "c")).reshape(lax.axis_size(("y", "c")), -1, hid)
-    line_terms = spread(added(ring_terms), "zl")
+    line_terms = spread(added(ring_terms).astype(jnp.bfloat16), "zl")
     own_grad = added(line_terms.reshape((-1,) + ring_terms.shape[1:]))
     weight_grad = spread(own_grad, ("y", "c")).reshape(feat_width, hid)
     return (activated, weight_grad)

time: 158 us -> 158 us (level)
  no operation moved by 1% of the time
where the time goes in v8:
time: 158 us
  blocking collectives  112 us (71%)
  starting transfers between devices  29.4 us (19%)
  Pallas kernels  6.98 us (4%)
  local copies, waits for them, and re-layouts  3.22 us (2%)
  matrix products  2.28 us (1%)
  waiting for transfers between devices  1.78 us (1%)
    all_to_all x7, blocking collectives, exchange(): return lax.all_to_all(pieces, axes, split_axis=0, concat_axis=0, tiled=True)  112 us
    ppermute x1, starting transfers between devices, on_device(): far = lax.ppermute(near, 'zh', [(0, 1), (1, 0)])  22.2 us
    ppermute x1, starting transfers between devices, on_device(): other_core = lax.ppermute(same_core, 'c', [(0, 1), (1, 0)])  6.54 us
    pallas_call x2, Pallas kernels, pick_parts(): pl.pallas_call(pick_kernel, out_shape=jax.ShapeDtypeStruct((count,) + par...  5 us
  transfers between devices with their start and end apart: 3, of which 2 were waited for; matrix products, arithmetic and copies ran while one was open for 0% of the time, Pallas kernels for 3%

profile of v8, /device:TPU:1, one launch (start us, length us, event | category | flops | bytes accessed | tf_op | source)
XLA Modules:
  0.0 157.5 jit_solution(3199537747978186513)
XLA Ops:
  0.6 0.0 copy-start
  0.7 0.9 constant_dynamic-slice_fusion
  1.6 20.9 %all_to_all.43 = bf16[6,96,128]{2,1,0:T(8,128)(2,1)S(1)} all-to-all(bf16[6,96,128]{2,1,0:T(8,128)(2,1)S(1)} %broadcast_in_dim.14), channel_id=1, replica_groups=mesh['zh'=2,'x'=4,'y'=8,'zl'=6,'c'=2] {'zl'}, dimensions={0} | all-to-all | bytes 294912 | tf_op jit(solution)/shard_map/all_to_all | solution.py:17
  22.5 0.2 broadcast_in_dim.15
  22.7 34.6 %all_to_all.44 = bf16[8,6,96,128]{3,2,1,0:T(8,128)(2,1)} all-to-all(bf16[8,6,96,128]{3,2,1,0:T(8,128)(2,1)S(1)} %broadcast_in_dim.15), channel_id=1, replica_groups=mesh['zh'=2,'x'=4,'y'=8,'zl'=6,'c'=2] {'y'}, dimensions={0} | all-to-all | bytes 2359296 | tf_op jit(solution)/shard_map/all_to_all | solution.py:17
  57.3 6.5 %collective-permute-start = (bf16[1152,4,128]{2,1,0:T(4,128)(2,1)}, bf16[1152,4,128]{2,1,0:T(4,128)(2,1)}, u32[]{:S(2)}, u32[]{:S(2)}) collective-permute-start(bf16[1152,4,128]{2,1,0:T(4,128)(2,1)} %bitcast.3.first_ref), channel_id=1, source_target_pairs={{0,1},{1,0},{2,3},{3,2},{4,5},{5,4},{6,7},{7,6},{8,9},{9,8},{10,11... | collective-permute-start | bytes 3538952 | tf_op jit(solution)/shard_map/ppermute | solution.py:162
  64.5 2.0 %shard_map.86 = (s32[24,24]{1,0:T(8,128)}, s32[24,24]{1,0:T(8,128)}) custom-call(s32[1]{0:T(128)} %bitcast.group_ref, s32[1]{0:T(128)} %bitcast.1.core_ref, s32[1]{0:T(128)S(6)} %copy.10.live_ref, s32[1,24]{1,0:T(1,128)} %column_ref.1, s32[48,96]{1,0:T(8,128)} %bitcast.32, s32[1,24]{1,0:T(1,128)} %column_ref.1), custom_call_target="tpu_custom_call" | custom-call | flops 4000000 | bytes 50000 | tf_op jit(solution)/shard_map/pallas_call | solution.py:97
  66.5 0.2 collective-permute-done.second_ref
  66.6 0.0 copy-start.2
  66.6 0.7 copy-done.2
  67.3 2.5 %shard_map.88 = bf16[576,4,128]{2,1,0:T(4,128)(2,1)S(1)} custom-call(s32[24,24]{1,0:T(8,128)S(1)} %copy-done.2, bf16[1152,4,128]{2,1,0:T(4,128)(2,1)} %bitcast.3.first_ref, bf16[1152,4,128]{2,1,0:T(4,128)(2,1)} %collective-permute-done.second_ref), custom_call_target="tpu_custom_call" | custom-call | flops 1000000 | bytes 3000000 | tf_op jit(solution)/shard_map/pallas_call | solution.py:132
  69.8 0.7 collective-permute-start.1
  70.6 0.0 copy-start.1
  70.6 0.7 copy-done.1
  71.3 2.5 %shard_map.87 = bf16[576,4,128]{2,1,0:T(4,128)(2,1)S(1)} custom-call(s32[24,24]{1,0:T(8,128)S(1)} %copy-done.1, bf16[1152,4,128]{2,1,0:T(4,128)(2,1)} %bitcast.3.first_ref, bf16[1152,4,128]{2,1,0:T(4,128)(2,1)} %collective-permute-done.second_ref), custom_call_target="tpu_custom_call" | custom-call | flops 1000000 | bytes 3000000 | tf_op jit(solution)/shard_map/pallas_call | solution.py:132
  73.8 0.0 copy-start.4
  73.8 0.0 collective-permute-done.1
  73.8 0.3 add.114
  74.1 0.0 copy-done
  74.1 0.7 fusion
  74.8 0.0 copy-start.3
  74.8 9.2 %all_to_all.45 = bf16[4,32,768]{2,1,0:T(8,128)(2,1)S(1)} all-to-all(bf16[4,32,768]{2,1,0:T(8,128)(2,1)S(1)} %bitcast.28), channel_id=1, replica_groups=mesh['zh'=2,'x'=4,'y'=8,'zl'=6,'c'=2] {'x'}, dimensions={0} | all-to-all | bytes 393216 | tf_op jit(solution)/shard_map/all_to_all | solution.py:17
  84.1 22.2 %collective-permute-start.2 = (bf16[32,768]{1,0:T(8,128)(2,1)S(1)}, bf16[32,768]{1,0:T(8,128)(2,1)S(1)}, u32[]{:S(2)}, u32[]{:S(2)}) collective-permute-start(bf16[32,768]{1,0:T(8,128)(2,1)S(1)} %fusion.2), channel_id=1, source_target_pairs={{0,384},{384,0},{1,385},{385,1},{2,386},{386,2},{3,387},{387,3},{4... | collective-permute-start | bytes 147464 | tf_op jit(solution)/shard_map/ppermute | solution.py:175
  106.3 1.6 %collective-permute-done.2 = bf16[32,768]{1,0:T(8,128)(2,1)S(1)} collective-permute-done((bf16[32,768]{1,0:T(8,128)(2,1)S(1)}, bf16[32,768]{1,0:T(8,128)(2,1)S(1)}, u32[]{:S(2)}, u32[]{:S(2)}) %collective-permute-start.2) | collective-permute-done | bytes 49184 | tf_op jit(solution)/shard_map/ppermute | solution.py:175
  108.0 7.5 %all_to_all.46 = bf16[4,32,768]{2,1,0:T(8,128)(2,1)S(1)} all-to-all(bf16[4,32,768]{2,1,0:T(8,128)(2,1)S(1)} %broadcast_in_dim.16), channel_id=1, replica_groups=mesh['zh'=2,'x'=4,'y'=8,'zl'=6,'c'=2] {'x'}, dimensions={0} | all-to-all | bytes 393216 | tf_op jit(solution)/shard_map/all_to_all | solution.py:17
  115.5 0.0 copy-done.4
  115.5 1.1 multiply_convert_fusion.1
  116.7 0.0 copy-done.3
  116.7 0.4 fusion.1
  117.1 14.7 %all_to_all.47 = bf16[16,8,256]{2,1,0:T(8,128)(2,1)S(1)} all-to-all(bf16[16,8,256]{2,1,0:T(8,128)(2,1)S(1)} %fusion.1), channel_id=1, replica_groups=mesh['zh'=2,'x'=4,'y'=8,'zl'=6,'c'=2] {'y','c'}, dimensions={0} | all-to-all | bytes 131072 | tf_op jit(solution)/shard_map/all_to_all | solution.py:17
  131.9 11.8 %all_to_all.48 = bf16[6,8,256]{2,1,0:T(8,128)(2,1)S(1)} all-to-all(bf16[6,8,256]{2,1,0:T(8,128)(2,1)S(1)} %broadcast_in_dim.18), channel_id=1, replica_groups=mesh['zh'=2,'x'=4,'y'=8,'zl'=6,'c'=2] {'zl'}, dimensions={0} | all-to-all | bytes 49152 | tf_op jit(solution)/shard_map/all_to_all | solution.py:17
  143.7 13.2 %all_to_all.49 = f32[16,8,256]{2,1,0:T(8,128)S(1)} all-to-all(f32[16,8,256]{2,1,0:T(8,128)S(1)} %broadcast_in_dim.40), channel_id=1, replica_groups=mesh['zh'=2,'x'=4,'y'=8,'zl'=6,'c'=2] {'y','c'}, dimensions={0} | all-to-all | bytes 262144 | tf_op jit(solution)/shard_map/all_to_all | solution.py:17
  156.9 0.7 copy.11
  (8 shorter events, 0.1 us)
Async XLA Ops:
  0.6 73.5 %copy-start = (bf16[24,96,768]{2,1,0:T(8,128)(2,1)S(1)}, bf16[24,96,768]{2,1,0:T(8,128)(2,1)}, u32[]{:S(2)}) copy-start(bf16[24,96,768]{2,1,0:T(8,128)(2,1)} %param.9) | copy-start | bytes 10616836
  57.3 9.3 %collective-permute-start = (bf16[1152,4,128]{2,1,0:T(4,128)(2,1)}, bf16[1152,4,128]{2,1,0:T(4,128)(2,1)}, u32[]{:S(2)}, u32[]{:S(2)}) collective-permute-start(bf16[1152,4,128]{2,1,0:T(4,128)(2,1)} %bitcast.3.first_ref), channel_id=1, source_target_pairs={{0,1},{1,0},{2,3},{3,2},{4,5},{5,4},{6,7},{7,6},{8,9},{9,8},{10,11... | collective-permute-start | bytes 3538952 | tf_op jit(solution)/shard_map/ppermute | solution.py:162
  66.6 0.7 copy-start.2
  69.8 3.9 %collective-permute-start.1 = (bf16[576,4,128]{2,1,0:T(4,128)(2,1)S(1)}, bf16[576,4,128]{2,1,0:T(4,128)(2,1)S(1)}, u32[]{:S(2)}, u32[]{:S(2)}) collective-permute-start(bf16[576,4,128]{2,1,0:T(4,128)(2,1)S(1)} %shard_map.88), channel_id=1, source_target_pairs={{576,672},{672,576},{577,673},{673,577},{578,674},{674,578},{579,6... | collective-permute-start | bytes 1769480 | tf_op jit(solution)/shard_map/ppermute | solution.py:164
  70.6 0.7 copy-start.1
  73.8 41.7 %copy-start.4 = (bf16[128,256]{1,0:T(8,128)(2,1)S(1)}, bf16[128,256]{1,0:T(8,128)(2,1)}, u32[]{:S(2)}) copy-start(bf16[128,256]{1,0:T(8,128)(2,1)} %param.13) | copy-start | bytes 196612
  74.8 41.8 %copy-start.3 = (bf16[768,256]{1,0:T(8,128)(2,1)S(1)}, bf16[768,256]{1,0:T(8,128)(2,1)}, u32[]{:S(2)}) copy-start(bf16[768,256]{1,0:T(8,128)(2,1)} %param.12) | copy-start | bytes 1179652
  84.1 23.8 %collective-permute-start.2 = (bf16[32,768]{1,0:T(8,128)(2,1)S(1)}, bf16[32,768]{1,0:T(8,128)(2,1)S(1)}, u32[]{:S(2)}, u32[]{:S(2)}) collective-permute-start(bf16[32,768]{1,0:T(8,128)(2,1)S(1)} %fusion.2), channel_id=1, source_target_pairs={{0,384},{384,0},{1,385},{385,1},{2,386},{386,2},{3,387},{387,3},{4... | collective-permute-start | bytes 147464 | tf_op jit(solution)/shard_map/ppermute | solution.py:175
